TPU v7x, 256 devices: a whole 4x4x8 slice. The times are simulated.
256 devices in a mesh: space: 32 (over z_lo, x, core), filt: 8 (over z_hi, y).
Axes of the slice: x: 4, y: 4, z: 8 (z_hi: 2, z_lo: 4; z = z_hi * 4 + z_lo), core: 2. Of those that a mesh axis runs over, the one named last changes fastest.
Arguments:
- activations: bfloat16 [64, 32, 56, 128], P('filt', 'space'), may hold values from -6 to 6
- kernel: bfloat16 [64, 64, 3, 3, 3], P('filt'), may hold values from -0.15625 to 0.15625
- preact: bfloat16 [64, 32, 56, 128], P('filt', 'space'), may hold values from -6 to 6
- upstream: bfloat16 [64, 32, 56, 128], P('filt', 'space'), may hold values from -6 to 6
Outputs:
- input_grad: bfloat16 [64, 32, 56, 128], P('filt', 'space')
- kernel_grad: float32 [64, 64, 3, 3, 3], P('filt')
All inputs are finite; a program needn't handle non-finite values.
Results may differ from a plain program's by a relative error of at most 0.0015.
Values may be sent and summed in bfloat16 or wider, within the bound.
No kernel may reach another device: no remote copies, remote signals or barrier semaphores. Data moves between devices by JAX's collectives and lax.ppermute only.
A program may use at most 128 MiB of HBM per device.

v0:
```python
import jax
import jax.numpy as jnp
from jax import lax
from jax.sharding import PartitionSpec as P


def with_halo(block, sides, width):
    for axis, dim in sides:
        count = lax.axis_size(axis)
        forward = [(i, i + 1) for i in range(count - 1)]
        backward = [(target, source) for source, target in forward]
        low = lax.ppermute(
            lax.slice_in_dim(block, block.shape[dim] - width, None, axis=dim), axis, forward
        )
        high = lax.ppermute(lax.slice_in_dim(block, 0, width, axis=dim), axis, backward)
        block = jnp.concatenate([low, block, high], axis=dim)
    return block


def pad_plane(volume):
    return jnp.pad(volume, ((0, 0), (0, 0), (1, 1), (1, 1)))


def data_grad(grad_pad, weight):
    chans = weight.shape[1]
    depth = grad_pad.shape[1] - 2
    rows = grad_pad.shape[2] - 2
    cols = grad_pad.shape[3] - 2
    total = jnp.zeros((chans, depth, rows, cols), jnp.float32)
    for depth_off in range(3):
        for row_off in range(3):
            for col_off in range(3):
                piece = grad_pad[
                    :,
                    2 - depth_off : 2 - depth_off + depth,
                    2 - row_off : 2 - row_off + rows,
                    2 - col_off : 2 - col_off + cols,
                ]
                total = total + jnp.einsum(
                    "fc,fzyx->czyx",
                    weight[:, :, depth_off, row_off, col_off],
                    piece,
                    preferred_element_type=jnp.float32,
                )
    return total


def weight_grad(grad, input_pad):
    depth, rows, cols = (grad.shape[1], grad.shape[2], grad.shape[3])
    terms = []
    for depth_off in range(3):
        for row_off in range(3):
            for col_off in range(3):
                piece = input_pad[
                    :,
                    depth_off : depth_off + depth,
                    row_off : row_off + rows,
                    col_off : col_off + cols,
                ]
                terms.append(
                    jnp.einsum("fzyx,czyx->fc", grad, piece, preferred_element_type=jnp.float32)
                )
    stacked = jnp.stack(terms, axis=-1)
    return stacked.reshape(grad.shape[0], input_pad.shape[0], 3, 3, 3)


def on_device(activations, kernel, preact, upstream):
    masked = jnp.where(preact > 0, upstream, jnp.zeros_like(upstream))
    depth = activations.shape[1]
    volume = lax.axis_size("space") * depth * activations.shape[2] * activations.shape[3]
    scale = 1.0 / jnp.sqrt(jnp.float32(volume))
    grad_halo = with_halo(masked, (("space", 1),), 1)
    every_chan = lax.all_gather(activations, "filt", axis=0, tiled=True)
    input_halo = with_halo(every_chan, (("space", 1),), 1)
    partial_grad = data_grad(pad_plane(grad_halo), kernel)
    input_grad = lax.psum_scatter(partial_grad, "filt", scatter_dimension=0, tiled=True).astype(
        jnp.bfloat16
    )
    local_terms = weight_grad(masked, pad_plane(input_halo))
    kernel_grad = lax.psum(local_terms, "space") * scale
    return (input_grad, kernel_grad)


def solution(mesh):
    in_specs = (
        P("filt", "space", None, None),
        P("filt", None, None, None, None),
        P("filt", "space", None, None),
        P("filt", "space", None, None),
    )
    out_specs = (P("filt", "space", None, None), P("filt", None, None, None, None))
    return jax.shard_map(
        on_device, mesh=mesh, in_specs=in_specs, out_specs=out_specs, check_vma=False
    )
```

profile of v0, /device:TPU:0, one launch (start us, length us, event | category | flops | bytes accessed | tf_op | source)
XLA Modules:
  0.0 298.2 jit_solution(15886607002823328554)
XLA Ops:
  7.2 0.9 copy.8
  8.1 50.3 %all_gather.3 = bf16[64,1,56,128]{3,0,2,1:T(8,128)(2,1)S(1)} all-gather(bf16[8,1,56,128]{3,0,2,1:T(8,128)(2,1)S(1)} %copy.8), channel_id=1, replica_groups=mesh['space'=32,'filt'=8] {'filt'}, dimensions={0}, use_global_device_ids=true | all-gather | bytes 1032192 | tf_op jit(solution)/shard_map/all_gather | solution.py:73
  58.5 2.4 collective-permute-start.2
  60.8 1.3 collective-permute-start.3
  62.1 1.0 compare_select_fusion
  63.1 3.8 %collective-permute-start = (bf16[8,1,56,128]{3,0,2,1:T(8,128)(2,1)S(1)}, bf16[8,1,56,128]{3,0,2,1:T(8,128)(2,1)S(1)}, u32[]{:S(2)}, u32[]{:S(2)}) collective-permute-start(bf16[8,1,56,128]{3,0,2,1:T(8,128)(2,1)S(1)} %compare_select_fusion), channel_id=1, source_target_pairs={{0,8},{8,16},{16,24},{24,32},{32,40},{40,48},{48,56},{56,64},{64,7... | collective-permute-start | bytes 344072 | tf_op jit(solution)/shard_map/ppermute | solution.py:12
  66.9 1.3 collective-permute-start.1
  68.2 1.1 fusion.68
  69.4 2.0 collective-permute-done.1
  72.2 0.5 fusion.17
  72.6 1.7 fusion.18
  74.4 1.7 fusion.19
  76.1 1.7 fusion.20
  77.8 1.7 fusion.21
  79.4 1.7 fusion.22
  81.2 1.8 fusion.23
  82.9 1.7 fusion.24
  84.6 1.7 fusion.25
  86.3 1.7 fusion.26
  88.0 1.7 fusion.27
  89.7 1.7 fusion.28
  91.4 1.6 fusion.29
  93.1 1.7 fusion.30
  94.8 1.7 fusion.31
  96.6 1.8 fusion.32
  98.3 1.7 fusion.33
  100.1 1.7 fusion.34
  101.7 1.7 fusion.35
  103.5 1.7 fusion.36
  105.1 1.7 fusion.37
  106.8 1.7 fusion.38
  108.5 1.7 fusion.39
  110.2 1.7 fusion.70
  111.9 16.2 %fusion.6 = f32[64,1,56,128]{3,0,2,1:T(8,128)} fusion(f32[56,128,64]{1,2,0:T(8,128)S(1)} %fusion.16, f32[56,128,64]{1,2,0:T(8,128)S(1)} %fusion.17, f32[56,128,64]{1,2,0:T(8,128)} %fusion.18, f32[56,128,64]{1,2,0:T(8,128)} %fusion.19, f32[56,128,64]{1,2,0:T(8,128)} %fusion.20, f32[56,128,64]{1,2,0:T(8,128)} %fusion.21, f32[56,128,64]{1,2,0:T(8,128)} %fusion.22, ...), kind=kOutput, calls=%fused_computation.17 | convolution fusion | flops 19267584 | bytes 49661952 | tf_op jit(solution)/shard_map/fc,fzyx->czyx/dot_general | solution.py:39
  128.1 5.1 %select_maximum_fusion = bf16[64,3,58,130]{3,0,2,1:T(8,128)(2,1)S(1)} fusion(bf16[64,1,56,128]{3,0,2,1:T(8,128)(2,1)} %collective-permute-done.3, bf16[64,1,56,128]{3,0,2,1:T(8,128)(2,1)S(1)} %all_gather.3, bf16[64,1,56,128]{3,0,2,1:T(8,128)(2,1)} %collective-permute-done.2), kind=kLoop, calls=%fused_computation.7 | loop fusion | flops 27505920 | bytes 5647872 | tf_op jit(solution)/shard_map/concatenate | solution.py:16
  134.0 0.5 convolution_dynamic-update-slice_fusion.24
  134.9 1.5 convolution_dynamic-update-slice_fusion.22
  136.4 0.5 convolution_dynamic-update-slice_fusion.21
  137.7 0.5 convolution_dynamic-update-slice_fusion.18
  139.1 0.5 convolution_dynamic-update-slice_fusion.15
  141.6 0.5 convolution_dynamic-update-slice_fusion.9
  142.9 0.5 convolution_dynamic-update-slice_fusion.6
  143.8 1.5 convolution_dynamic-update-slice_fusion.4
  146.6 0.5 convolution_dynamic-update-slice_fusion
  147.1 142.0 %psum.7 = f32[8,64,3,3,3]{1,0,4,3,2:T(8,128)S(1)} all-reduce(f32[8,64,3,3,3]{1,0,4,3,2:T(8,128)S(1)} %bitcast.423), channel_id=1, replica_groups=mesh['space'=32,'filt'=8] {'space'}, use_global_device_ids=true, to_apply=%region_1.2 | all-reduce | flops 13824 | bytes 110592 | tf_op jit(solution)/shard_map/psum | solution.py:80
  289.1 0.7 broadcast_multiply_fusion
  289.8 1.0 convert_element_type.7
  290.7 0.7 copy.9
  (28 shorter events, 8.2 us)
Async XLA Ops:
  7.2 282.6 %reduce-scatter.2.cloned.1.call-start = ((), (), s32[]{:S(2)}) async-start(), calls=%async_computation.1 | async-start | bytes 2064384 | tf_op jit(solution)/shard_map/reduce_scatter | solution.py:76
  58.5 13.3 %copy-start = (bf16[8,64,3,3,3]{1,0,4,3,2:T(8,128)(2,1)S(1)}, bf16[8,64,3,3,3]{1,0,4,3,2:T(8,128)(2,1)}, u32[]{:S(2)}) copy-start(bf16[8,64,3,3,3]{1,0,4,3,2:T(8,128)(2,1)} %param.5) | copy-start | bytes 82948
  58.5 69.6 %collective-permute-start.2 = (bf16[64,1,56,128]{3,0,2,1:T(8,128)(2,1)S(1)}, bf16[64,1,56,128]{3,0,2,1:T(8,128)(2,1)}, u32[]{:S(2)}, u32[]{:S(2)}) collective-permute-start(bf16[64,1,56,128]{3,0,2,1:T(8,128)(2,1)S(1)} %all_gather.3), channel_id=1, source_target_pairs={{0,8},{8,16},{16,24},{24,32},{32,40},{40,48},{48,56},{56,64},{64,7... | collective-permute-start | bytes 2752520 | tf_op jit(solution)/shard_map/ppermute | solution.py:12
  60.8 67.3 %collective-permute-start.3 = (bf16[64,1,56,128]{3,0,2,1:T(8,128)(2,1)S(1)}, bf16[64,1,56,128]{3,0,2,1:T(8,128)(2,1)}, u32[]{:S(2)}, u32[]{:S(2)}) collective-permute-start(bf16[64,1,56,128]{3,0,2,1:T(8,128)(2,1)S(1)} %all_gather.3), channel_id=1, source_target_pairs={{8,0},{16,8},{24,16},{32,24},{40,32},{48,40},{56,48},{64,56},{72,6... | collective-permute-start | bytes 2752520 | tf_op jit(solution)/shard_map/ppermute | solution.py:15
  63.1 6.2 %collective-permute-start = (bf16[8,1,56,128]{3,0,2,1:T(8,128)(2,1)S(1)}, bf16[8,1,56,128]{3,0,2,1:T(8,128)(2,1)S(1)}, u32[]{:S(2)}, u32[]{:S(2)}) collective-permute-start(bf16[8,1,56,128]{3,0,2,1:T(8,128)(2,1)S(1)} %compare_select_fusion), channel_id=1, source_target_pairs={{0,8},{8,16},{16,24},{24,32},{32,40},{40,48},{48,56},{56,64},{64,7... | collective-permute-start | bytes 344072 | tf_op jit(solution)/shard_map/ppermute | solution.py:12
  66.9 4.5 %collective-permute-start.1 = (bf16[8,1,56,128]{3,0,2,1:T(8,128)(2,1)S(1)}, bf16[8,1,56,128]{3,0,2,1:T(8,128)(2,1)S(1)}, u32[]{:S(2)}, u32[]{:S(2)}) collective-permute-start(bf16[8,1,56,128]{3,0,2,1:T(8,128)(2,1)S(1)} %compare_select_fusion), channel_id=1, source_target_pairs={{8,0},{16,8},{24,16},{32,24},{40,32},{48,40},{56,48},{64,56},{72,6... | collective-permute-start | bytes 344072 | tf_op jit(solution)/shard_map/ppermute | solution.py:15
Sparse Core Ops, SparseCore 0:
  128.2 99.9 reduce-scatter.1
where the time goes:
time: 299 us; the launch traced here: 298 us
  blocking collectives  192 us (64%)
  matrix products  71.3 us (24%)
  between operations  14.2 us (5%)
  starting transfers between devices  8.81 us (3%)
  other arithmetic  8.03 us (3%)
    psum x1, blocking collectives, on_device(): kernel_grad = lax.psum(local_terms, 'space') * scale  142 us
    dot_general x27, matrix products, data_grad(): jnp.einsum('fc,fzyx->czyx', weight[:, :, depth_off, row_off, col_off], pi...  57.4 us
    all_gather x1, blocking collectives, on_device(): every_chan = lax.all_gather(activations, 'filt', axis=0, tiled=True)  50.3 us
    dot_general x27, matrix products, weight_grad(): jnp.einsum('fzyx,czyx->fc', grad, piece, preferred_element_type=jnp.float32)  13.8 us
    ppermute x2, starting transfers between devices, with_halo(): lax.ppermute(lax.slice_in_dim(block, block.shape[dim] - width, None, axis...  6.2 us
  transfers between devices with their start and end apart: 5, of which 1 were waited for; matrix products, arithmetic and copies ran while one was open for 26% of the time, Pallas kernels for 0%

commit v1 on v0

v1 whole, which is shorter than its diff:
```python
import jax
import jax.numpy as jnp
from jax import lax
from jax.experimental import pallas as pl
from jax.experimental.pallas import tpu as pltpu
from jax.sharding import PartitionSpec as P

ROWS, COLS, CH = 56, 128, 8
BF, F32 = jnp.bfloat16, jnp.float32


def space_pairs(to):
    pairs = []
    for i in range(32):
        z, x, core = to(i >> 3, (i >> 1) & 3, i & 1)
        pairs.append((i, ((z % 4) * 4 + x % 4) * 2 + core))
    return pairs


def filt_pairs(to):
    pairs = []
    for i in range(8):
        h, y = to(i >> 2, i & 3)
        pairs.append((i, h * 4 + y % 4))
    return pairs


UP = [(i, i + 1) for i in range(31)]
DOWN = [(i + 1, i) for i in range(31)]
CORE = space_pairs(lambda z, x, core: (z, x, core ^ 1))
X_OTHERS = [space_pairs(lambda z, x, core, j=j: (z, x + j, core)) for j in (1, 3, 2)]
Z_OTHERS = [space_pairs(lambda z, x, core, j=j: (z ^ j, x, core)) for j in (1, 2, 3)]
HALF = filt_pairs(lambda h, y: (h ^ 1, y))
Y_OTHERS = [filt_pairs(lambda h, y, j=j: (h, y + j)) for j in (1, 3, 2)]
Y_BACK = [filt_pairs(lambda h, y, j=j: (h, y - j)) for j in (1, 3, 2)]


def place():
    space, filt = lax.axis_index("space"), lax.axis_index("filt")
    return space % 2, filt // 4, filt % 4


def params():
    return pltpu.CompilerParams(vmem_limit_bytes=40 * 1024 * 1024)


def whole(count):
    return [pl.BlockSpec(memory_space=pltpu.VMEM)] * count


def mask_body(pre_ref, up_ref, kern_ref, out_ref):
    for f in range(CH):
        keep = pre_ref[f].astype(F32) > 0
        out_ref[f] = jnp.where(keep, up_ref[f].astype(F32), 0.0).astype(BF)
    blank = jnp.zeros((CH, 64), F32)
    for plane in range(2):
        pieces = []
        for k2 in range(7 * plane, 7 * plane + 7):
            even = kern_ref[2 * k2].astype(F32)
            odd = kern_ref[2 * k2 + 1].astype(F32) if 2 * k2 + 1 < 27 else blank
            pieces.append(jnp.concatenate([even, odd], axis=1))
        out_ref[CH + plane] = jnp.concatenate(pieces, axis=0).astype(BF)


def mask_call(preact, upstream, kern):
    return pl.pallas_call(
        mask_body,
        out_shape=jax.ShapeDtypeStruct((CH + 2, ROWS, COLS), BF),
        in_specs=whole(3),
        out_specs=pl.BlockSpec(memory_space=pltpu.VMEM),
        compiler_params=params(),
        cost_estimate=pl.CostEstimate(flops=100_000, bytes_accessed=500_000, transcendentals=0),
        name="mask",
    )(preact, upstream, kern)


def spread(ref, planes, scratch):
    for ch in range(planes):
        scratch[pl.ds(ch * ROWS, ROWS), :] = ref[ch].astype(F32)


def row_of(scratch, row):
    return scratch[pl.ds(row, CH, stride=ROWS), :]


def column_shifts(scratch, row, lane):
    block = row_of(scratch, row)
    left = jnp.where(lane == COLS - 1, 0.0, pltpu.roll(block, COLS - 1, 1))
    right = jnp.where(lane == 0, 0.0, pltpu.roll(block, 1, 1))
    return [left, block, right]


def shifted_rows(scratches, rows, lane):
    columns = []
    for row in rows:
        pieces = []
        for scratch in scratches:
            pieces += column_shifts(scratch, row, lane)
        columns.append(jnp.concatenate(pieces, axis=0).astype(BF))
    return jnp.concatenate(columns, axis=1)


def weight_body(m0, m1, m2, m3, *refs):
    acts, (keep_ref, send_ref), scratch = refs[:6], refs[6:8], refs[8:]
    core, _, _ = place()
    masked, planes = scratch[:4], scratch[4:]
    for ref, buf in zip((m0, m1, m2, m3), masked):
        spread(ref, CH, buf)
    for ref, buf in zip(acts, planes):
        spread(ref, CH, buf)
    lane = lax.broadcasted_iota(jnp.int32, (CH, COLS), 1)
    zero = jnp.zeros((CH, COLS), F32)
    gap = jnp.zeros((COLS - 9 * CH, COLS), F32)
    total = jnp.zeros((96, 256), F32)
    step = 8
    for first in range(0, ROWS, step):
        rows = range(first, first + step)
        lhs = shifted_rows(masked, rows, lane)
        columns = []
        for row in rows:
            pieces = []
            for block in range(2):
                for kz in range(3):
                    for ky in range(3):
                        at = row + ky - 1
                        inside = 0 <= at < ROWS
                        pieces.append(row_of(planes[3 * block + kz], at) if inside else zero)
                pieces.append(gap)
            columns.append(jnp.concatenate(pieces, axis=0).astype(BF))
        rhs = jnp.concatenate(columns, axis=1)
        total = total + lax.dot_general(
            lhs, rhs, (((1,), (1,)), ((), ())), preferred_element_type=F32
        )
    own, other = total[:, :COLS], total[:, COLS:]
    first_core = core == 0
    keep_ref[...] = jnp.where(first_core, own, other)
    send_ref[...] = jnp.where(first_core, other, own)


def weight_call(masked, acts):
    shape = jax.ShapeDtypeStruct((96, COLS), F32)
    return pl.pallas_call(
        weight_body,
        out_shape=(shape, shape),
        in_specs=whole(10),
        out_specs=tuple(whole(2)),
        scratch_shapes=[pltpu.VMEM((CH * ROWS, COLS), F32)] * 10,
        compiler_params=params(),
        cost_estimate=pl.CostEstimate(
            flops=2 * 96 * 256 * 7168, bytes_accessed=1_500_000, transcendentals=0
        ),
        name="weight_grad",
    )(*masked, *acts)


def data_body(m0, m1, m2, m3, down_ref, mid_ref, up_ref, *masked):
    _, half, y = place()
    for ref, buf in zip((m0, m1, m2, m3), masked):
        spread(ref, CH, buf)
    lane = lax.broadcasted_iota(jnp.int32, (CH, COLS), 1)
    rows = []
    for ref in (m0, m1, m2, m3):
        parts = [ref[CH].astype(F32), ref[CH + 1].astype(F32)]
        for kx in range(3):
            sums = [jnp.zeros((CH, COLS), F32) for _ in range(2)]
            for q in range(9):
                k = 3 * q + kx
                pair, odd = k // 2, k % 2
                value = parts[pair // 7][(pair % 7) * CH : (pair % 7 + 1) * CH]
                for block in range(2):
                    start = 8 * (4 * (half ^ block) + y)
                    shift = lax.rem(8 * q + 256 - 64 * odd - start, 128)
                    moved = pltpu.roll(value, shift, 1)
                    here = (lane >= 8 * q) & (lane < 8 * q + 8)
                    sums[block] = jnp.where(here, moved, sums[block])
            rows.append(jnp.concatenate(sums, axis=1))
    weights = jnp.concatenate(rows + [jnp.zeros((32, 256), F32)], axis=0)
    weights = jnp.transpose(weights)
    weights = jnp.concatenate([weights[:72, :96], weights[128:200, :96]], axis=0).astype(BF)
    outs = (down_ref, mid_ref, up_ref)
    sums = {}
    step = 4
    for first in range(0, ROWS, step):
        got = jnp.dot(
            weights, shifted_rows(masked, range(first, first + step), lane), preferred_element_type=F32
        )
        for i in range(step):
            row = first + i
            for block in range(2):
                for kz in range(3):
                    for ky in range(3):
                        at = row + ky - 1
                        if not 0 <= at < ROWS:
                            continue
                        top = ((block * 3 + kz) * 3 + ky) * CH
                        term = got[top : top + CH, i * COLS : (i + 1) * COLS]
                        key = (block, kz, at)
                        sums[key] = sums[key] + term if key in sums else term
                    done = [row - 1] if row < ROWS - 1 else [row - 1, row]
                    for at in done:
                        if at >= 0:
                            outs[kz][pl.ds(block * CH * ROWS + at, CH, stride=ROWS), :] = sums.pop(
                                (block, kz, at)
                            )


def data_call(masked):
    shape = jax.ShapeDtypeStruct((2 * CH * ROWS, COLS), F32)
    return pl.pallas_call(
        data_body,
        out_shape=(shape, shape, shape),
        in_specs=whole(4),
        out_specs=tuple(whole(3)),
        scratch_shapes=[pltpu.VMEM((CH * ROWS, COLS), F32)] * 4,
        compiler_params=params(),
        cost_estimate=pl.CostEstimate(
            flops=2 * 144 * 96 * 7168, bytes_accessed=2_000_000, transcendentals=0
        ),
        name="data_grad",
    )(*masked)


def final_body(scale, mine_ref, theirs_ref, out_ref):
    core, half, y = place()
    lane = lax.broadcasted_iota(jnp.int32, (24, COLS), 1)
    sources = []
    for ref, part in ((mine_ref, half ^ core), (theirs_ref, half ^ core ^ 1)):
        for j, away in enumerate((0, 1, 3, 2)):
            block = 4 * part + lax.rem(y + away, 4)
            sources.append((block, ref[24 * j : 24 * j + 24]))
    for q in range(9):
        total = jnp.zeros((24, COLS), F32)
        for block, value in sources:
            moved = pltpu.roll(value, lax.rem(8 * block + 128 - 8 * q, 128), 1)
            here = (lane >= 8 * block) & (lane < 8 * block + 8)
            total = jnp.where(here, moved, total)
        out_ref[24 * q : 24 * q + 24] = (total * scale)[:, :64]


def final_call(mine, theirs, scale):
    return pl.pallas_call(
        lambda *refs: final_body(scale, *refs),
        out_shape=jax.ShapeDtypeStruct((216, 64), F32),
        in_specs=whole(2),
        out_specs=pl.BlockSpec(memory_space=pltpu.VMEM),
        compiler_params=params(),
        cost_estimate=pl.CostEstimate(flops=100_000, bytes_accessed=200_000, transcendentals=0),
        name="place_blocks",
    )(mine, theirs)


def on_device(activations, kernel, preact, upstream):
    layers = lax.axis_size("space") * activations.shape[1]
    scale = (
        1.0 / float(layers * ROWS * COLS) ** 0.5
    )
    acts, pre, ups = (array[:, 0] for array in (activations, preact, upstream))
    kern = jnp.transpose(kernel, (2, 3, 4, 0, 1)).reshape(27, CH, 64)
    other = lax.ppermute(acts, "filt", HALF)
    mine = mask_call(pre, ups, kern)
    masked = [mine] + [lax.ppermute(mine, "filt", pairs) for pairs in Y_OTHERS]
    low, high = lax.ppermute(acts, "space", UP), lax.ppermute(acts, "space", DOWN)
    other_low, other_high = lax.ppermute(other, "space", UP), lax.ppermute(other, "space", DOWN)

    down, mid, up = data_call(masked)
    keep, send = weight_call(masked, (low, acts, high, other_low, other, other_high))

    terms = keep + lax.ppermute(send, "space", CORE)
    terms = sum([lax.ppermute(terms, "space", pairs) for pairs in X_OTHERS], terms)
    terms = sum([lax.ppermute(terms, "space", pairs) for pairs in Z_OTHERS], terms)
    blocks = [terms[24 * j : 24 * j + 24] for j in range(4)]
    got = [lax.ppermute(block, "filt", pairs) for block, pairs in zip(blocks[1:], Y_BACK)]
    mine_blocks = jnp.concatenate([blocks[0]] + got, axis=0)
    their_blocks = lax.ppermute(mine_blocks, "space", CORE)
    grads = final_call(mine_blocks, their_blocks, scale)
    kernel_grad = jnp.transpose(grads.reshape(3, 3, 3, CH, 64), (3, 4, 0, 1, 2))

    layer = mid + lax.ppermute(down, "space", DOWN) + lax.ppermute(up, "space", UP)
    own, away = layer[: CH * ROWS], layer[CH * ROWS :]
    own = own + lax.ppermute(away, "filt", HALF)
    input_grad = own.astype(BF).reshape(CH, 1, ROWS, COLS)
    return (input_grad, kernel_grad)


def solution(mesh):
    in_specs = (
        P("filt", "space", None, None),
        P("filt", None, None, None, None),
        P("filt", "space", None, None),
        P("filt", "space", None, None),
    )
    out_specs = (P("filt", "space", None, None), P("filt", None, None, None, None))
    return jax.shard_map(
        on_device, mesh=mesh, in_specs=in_specs, out_specs=out_specs, check_vma=False
    )
```

time: 299 us -> 71.8 us (0.24)
  the two profiles are of different devices: /device:TPU:0 before, /device:TPU:71 now
where the time goes in v1:
time: 71.8 us; the launch traced here: 71.5 us
  starting transfers between devices  43.5 us (61%)
  waiting for transfers between devices  20.6 us (29%)
  Pallas kernels  3.18 us (4%)
  local copies, waits for them, and re-layouts  2.63 us (4%)
  between operations  0.85 us (1%)
  other arithmetic  0.78 us (1%)
    ppermute x6, waiting for transfers between devices, on_device(): lax.ppermute(terms, 'space', pairs)  13.3 us
    ppermute x6, starting transfers between devices, on_device(): lax.ppermute(terms, 'space', pairs)  7.15 us
    ppermute x1, starting transfers between devices, on_device(): lax.ppermute(other, 'space', UP)  5.75 us
    ppermute x1, starting transfers between devices, on_device(): other = lax.ppermute(acts, 'filt', HALF)  5.2 us
    ppermute x1, starting transfers between devices, on_device(): lax.ppermute(acts, 'space', UP)  4.81 us
    ppermute x1, starting transfers between devices, on_device(): lax.ppermute(up, 'space', UP)  4.77 us
    ppermute x3, starting transfers between devices, on_device(): masked = [mine] + [lax.ppermute(mine, 'filt', pairs) for pairs in Y_OTHERS]  4.45 us
    ppermute x3, starting transfers between devices, on_device(): lax.ppermute(block, 'filt', pairs)  3.5 us
  transfers between devices with their start and end apart: 22, of which 9 were waited for; matrix products, arithmetic and copies ran while one was open for 0% of the time, Pallas kernels for 3%

profile of v1, /device:TPU:71, one launch (start us, length us, event | category | flops | bytes accessed | tf_op | source)
XLA Modules:
  0.0 71.5 jit_solution(15769019811295639014)
XLA Ops:
  0.6 5.2 %collective-permute-start.8 = (bf16[8,56,128]{2,1,0:T(8,128)(2,1)}, bf16[8,56,128]{2,1,0:T(8,128)(2,1)S(1)}, u32[]{:S(2)}, u32[]{:S(2)}) collective-permute-start(bf16[8,56,128]{2,1,0:T(8,128)(2,1)} %bitcast.15), channel_id=1, source_target_pairs={{0,4},{1,5},{2,6},{3,7},{4,0},{5,1},{6,2},{7,3},{8,12},{9,13},{10,... | collective-permute-start | bytes 344072 | tf_op jit(solution)/shard_map/ppermute | solution.py:259
  5.8 2.9 %collective-permute-start.7 = (bf16[8,56,128]{2,1,0:T(8,128)(2,1)}, bf16[8,56,128]{2,1,0:T(8,128)(2,1)S(1)}, u32[]{:S(2)}, u32[]{:S(2)}) collective-permute-start(bf16[8,56,128]{2,1,0:T(8,128)(2,1)} %bitcast.16), channel_id=1, source_target_pairs={{8,0},{16,8},{24,16},{32,24},{40,32},{48,40},{56,48},{64,56},{72,6... | collective-permute-start | bytes 344072 | tf_op jit(solution)/shard_map/ppermute | solution.py:262
  8.7 4.8 %collective-permute-start.6 = (bf16[8,56,128]{2,1,0:T(8,128)(2,1)}, bf16[8,56,128]{2,1,0:T(8,128)(2,1)S(1)}, u32[]{:S(2)}, u32[]{:S(2)}) collective-permute-start(bf16[8,56,128]{2,1,0:T(8,128)(2,1)} %bitcast.17), channel_id=1, source_target_pairs={{0,8},{8,16},{16,24},{24,32},{32,40},{40,48},{48,56},{56,64},{64,7... | collective-permute-start | bytes 344072 | tf_op jit(solution)/shard_map/ppermute | solution.py:262
  13.5 0.9 %copy-done = bf16[8,1,56,128]{3,2,1,0:T(8,128)(2,1)S(1)} copy-done((bf16[8,1,56,128]{3,2,1,0:T(8,128)(2,1)S(1)}, bf16[8,1,56,128]{3,2,1,0:T(8,128)(2,1)}, u32[]{:S(2)}) %copy-start) | copy-done | bytes 114712
  14.4 0.9 %copy-done.1 = bf16[8,1,56,128]{3,2,1,0:T(8,128)(2,1)S(1)} copy-done((bf16[8,1,56,128]{3,2,1,0:T(8,128)(2,1)S(1)}, bf16[8,1,56,128]{3,2,1,0:T(8,128)(2,1)}, u32[]{:S(2)}) %copy-start.1) | copy-done | bytes 114712
  15.3 0.8 %copy-done.2 = bf16[8,64,3,3,3]{1,0,4,3,2:T(8,128)(2,1)S(1)} copy-done((bf16[8,64,3,3,3]{1,0,4,3,2:T(8,128)(2,1)S(1)}, bf16[8,64,3,3,3]{1,0,4,3,2:T(8,128)(2,1)}, u32[]{:S(2)}) %copy-start.2) | copy-done | bytes 27672
  16.1 0.1 mask.1.m0
  16.2 3.0 %collective-permute-start.2 = (bf16[10,56,128]{2,1,0:T(8,128)(2,1)S(1)}, bf16[10,56,128]{2,1,0:T(8,128)(2,1)S(1)}, u32[]{:S(2)}, u32[]{:S(2)}) collective-permute-start(bf16[10,56,128]{2,1,0:T(8,128)(2,1)S(1)} %mask.1.m0), channel_id=1, source_target_pairs={{0,2},{1,3},{2,0},{3,1},{4,6},{5,7},{6,4},{7,5},{8,10},{9,11},{10,... | collective-permute-start | bytes 430088 | tf_op jit(solution)/shard_map/ppermute | solution.py:261
  19.2 0.8 %collective-permute-start.1 = (bf16[10,56,128]{2,1,0:T(8,128)(2,1)S(1)}, bf16[10,56,128]{2,1,0:T(8,128)(2,1)S(1)}, u32[]{:S(2)}, u32[]{:S(2)}) collective-permute-start(bf16[10,56,128]{2,1,0:T(8,128)(2,1)S(1)} %mask.1.m0), channel_id=1, source_target_pairs={{0,3},{1,0},{2,1},{3,2},{4,7},{5,4},{6,5},{7,6},{8,11},{9,8},{10,9... | collective-permute-start | bytes 430088 | tf_op jit(solution)/shard_map/ppermute | solution.py:261
  20.0 0.0 collective-permute-done.8.refs_4_
  20.0 0.7 collective-permute-start
  20.7 0.0 collective-permute-done.7.refs_2_
  20.7 1.9 %collective-permute-start.10 = (bf16[8,56,128]{2,1,0:T(8,128)(2,1)S(1)}, bf16[8,56,128]{2,1,0:T(8,128)(2,1)S(1)}, u32[]{:S(2)}, u32[]{:S(2)}) collective-permute-start(bf16[8,56,128]{2,1,0:T(8,128)(2,1)S(1)} %collective-permute-done.8.refs_4_), channel_id=1, source_target_pairs={{8,0},{16,8},{24,16},{32,24},{40,32},{48,40},{56,48},{64,56},{72,6... | collective-permute-start | bytes 344072 | tf_op jit(solution)/shard_map/ppermute | solution.py:263
  22.6 0.0 collective-permute-done.6.refs_0_
  22.6 5.8 %collective-permute-start.9 = (bf16[8,56,128]{2,1,0:T(8,128)(2,1)S(1)}, bf16[8,56,128]{2,1,0:T(8,128)(2,1)S(1)}, u32[]{:S(2)}, u32[]{:S(2)}) collective-permute-start(bf16[8,56,128]{2,1,0:T(8,128)(2,1)S(1)} %collective-permute-done.8.refs_4_), channel_id=1, source_target_pairs={{0,8},{8,16},{16,24},{24,32},{32,40},{40,48},{48,56},{56,64},{64,7... | collective-permute-start | bytes 344072 | tf_op jit(solution)/shard_map/ppermute | solution.py:263
  28.3 0.0 collective-permute-done.2.m3
  28.4 0.0 collective-permute-done.1.m2
  28.4 0.0 collective-permute-done.m1
  28.4 0.5 collective-permute-done.10.refs_5_
  28.9 1.2 %collective-permute-done.9.refs_3_ = bf16[8,56,128]{2,1,0:T(8,128)(2,1)S(1)} collective-permute-done((bf16[8,56,128]{2,1,0:T(8,128)(2,1)S(1)}, bf16[8,56,128]{2,1,0:T(8,128)(2,1)S(1)}, u32[]{:S(2)}, u32[]{:S(2)}) %collective-permute-start.9) | collective-permute-done | bytes 114720 | tf_op jit(solution)/shard_map/ppermute | solution.py:263
  30.1 1.2 %weight_grad.1 = (f32[96,128]{1,0:T(8,128)S(1)}, f32[96,128]{1,0:T(8,128)S(1)}) custom-call(bf16[10,56,128]{2,1,0:T(8,128)(2,1)S(1)} %mask.1.m0, bf16[10,56,128]{2,1,0:T(8,128)(2,1)S(1)} %collective-permute-done.m1, bf16[10,56,128]{2,1,0:T(8,128)(2,1)S(1)} %collective-permute-done.1.m2, bf16[10,56,128]{2,1,0:T(8,128)(2,1)S(1)} %collective-permute-done.2.m3, ...), custom_call_target="tpu_custom_call" | custom-call | flops 352321536 | bytes 1500000 | tf_op jit(solution)/shard_map/weight_grad/pallas_call | solution.py:142
  31.3 0.1 collective-permute-start.11
  31.4 1.2 %collective-permute-done.11 = f32[96,128]{1,0:T(8,128)S(1)} collective-permute-done((f32[96,128]{1,0:T(8,128)S(1)}, f32[96,128]{1,0:T(8,128)S(1)}, u32[]{:S(2)}, u32[]{:S(2)}) %collective-permute-start.11) | collective-permute-done | bytes 49184 | tf_op jit(solution)/shard_map/ppermute | solution.py:268
  32.6 0.1 collective-permute-start.14
  32.7 4.3 %collective-permute-start.13 = (f32[96,128]{1,0:T(8,128)S(1)}, f32[96,128]{1,0:T(8,128)S(1)}, u32[]{:S(2)}, u32[]{:S(2)}) collective-permute-start(f32[96,128]{1,0:T(8,128)S(1)} %add.33), channel_id=1, source_target_pairs={{0,48},{8,56},{16,0},{24,8},{32,16},{40,24},{48,32},{56,40},{64,11... | collective-permute-start | bytes 147464 | tf_op jit(solution)/shard_map/ppermute | solution.py:269
  37.0 0.0 collective-permute-start.12
  37.0 1.0 %data_grad.1 = (f32[896,128]{1,0:T(8,128)S(1)}, f32[896,128]{1,0:T(8,128)S(1)}, f32[896,128]{1,0:T(8,128)S(1)}) custom-call(bf16[10,56,128]{2,1,0:T(8,128)(2,1)S(1)} %mask.1.m0, bf16[10,56,128]{2,1,0:T(8,128)(2,1)S(1)} %collective-permute-done.m1, bf16[10,56,128]{2,1,0:T(8,128)(2,1)S(1)} %collective-permute-done.1.m2, ...), custom_call_target="tpu_custom_call" | custom-call | flops 198180864 | bytes 2000000 | tf_op jit(solution)/shard_map/data_grad/pallas_call | solution.py:209
  38.0 2.9 %collective-permute-start.3 = (f32[896,128]{1,0:T(8,128)S(1)}, f32[896,128]{1,0:T(8,128)S(1)}, u32[]{:S(2)}, u32[]{:S(2)}) collective-permute-start(f32[896,128]{1,0:T(8,128)S(1)} %get-tuple-element.8), channel_id=1, source_target_pairs={{8,0},{16,8},{24,16},{32,24},{40,32},{48,40},{56,48},{64,56},{72,6... | collective-permute-start | bytes 1376264 | tf_op jit(solution)/shard_map/ppermute | solution.py:278
  40.9 4.8 %collective-permute-start.4 = (f32[896,128]{1,0:T(8,128)S(1)}, f32[896,128]{1,0:T(8,128)S(1)}, u32[]{:S(2)}, u32[]{:S(2)}) collective-permute-start(f32[896,128]{1,0:T(8,128)S(1)} %get-tuple-element.9), channel_id=1, source_target_pairs={{0,8},{8,16},{16,24},{24,32},{32,40},{40,48},{48,56},{56,64},{64,7... | collective-permute-start | bytes 1376264 | tf_op jit(solution)/shard_map/ppermute | solution.py:278
  45.7 0.0 collective-permute-done.14
  45.7 0.0 collective-permute-done.13
  45.8 0.0 collective-permute-done.12
  45.8 0.8 %collective-permute-start.17 = (f32[96,128]{1,0:T(8,128)S(1)}, f32[96,128]{1,0:T(8,128)S(1)}, u32[]{:S(2)}, u32[]{:S(2)}) collective-permute-start(f32[96,128]{1,0:T(8,128)S(1)} %add_add_fusion.2), channel_id=1, source_target_pairs={{0,192},{8,200},{16,208},{24,216},{32,224},{40,232},{48,240},{56,2... | collective-permute-start | bytes 147464 | tf_op jit(solution)/shard_map/ppermute | solution.py:270
  46.6 0.0 collective-permute-start.16
  46.6 1.9 %collective-permute-start.15 = (f32[96,128]{1,0:T(8,128)S(1)}, f32[96,128]{1,0:T(8,128)S(1)}, u32[]{:S(2)}, u32[]{:S(2)}) collective-permute-start(f32[96,128]{1,0:T(8,128)S(1)} %add_add_fusion.2), channel_id=1, source_target_pairs={{0,64},{8,72},{16,80},{24,88},{32,96},{40,104},{48,112},{56,120},{... | collective-permute-start | bytes 147464 | tf_op jit(solution)/shard_map/ppermute | solution.py:270
  48.5 13.3 %collective-permute-done.17 = f32[96,128]{1,0:T(8,128)S(1)} collective-permute-done((f32[96,128]{1,0:T(8,128)S(1)}, f32[96,128]{1,0:T(8,128)S(1)}, u32[]{:S(2)}, u32[]{:S(2)}) %collective-permute-start.17) | collective-permute-done | bytes 49184 | tf_op jit(solution)/shard_map/ppermute | solution.py:270
  61.9 0.1 add_add_fusion
  62.0 0.1 collective-permute-start.5
  62.1 0.8 %collective-permute-start.20 = (f32[24,128]{1,0:T(8,128)S(1)}, f32[24,128]{1,0:T(8,128)S(1)}, u32[]{:S(2)}, u32[]{:S(2)}) collective-permute-start(f32[24,128]{1,0:T(8,128)S(1)} %get-tuple-element.15), channel_id=1, source_target_pairs={{0,2},{1,3},{2,0},{3,1},{4,6},{5,7},{6,4},{7,5},{8,10},{9,11},{10,... | collective-permute-start | bytes 36872 | tf_op jit(solution)/shard_map/ppermute | solution.py:272
  62.9 1.8 %collective-permute-start.19 = (f32[24,128]{1,0:T(8,128)S(1)}, f32[24,128]{1,0:T(8,128)S(1)}, u32[]{:S(2)}, u32[]{:S(2)}) collective-permute-start(f32[24,128]{1,0:T(8,128)S(1)} %get-tuple-element.16), channel_id=1, source_target_pairs={{0,1},{1,2},{2,3},{3,0},{4,5},{5,6},{6,7},{7,4},{8,9},{9,10},{10,1... | collective-permute-start | bytes 36872 | tf_op jit(solution)/shard_map/ppermute | solution.py:272
  64.7 0.9 %collective-permute-start.18 = (f32[24,128]{1,0:T(8,128)S(1)}, f32[24,128]{1,0:T(8,128)S(1)}, u32[]{:S(2)}, u32[]{:S(2)}) collective-permute-start(f32[24,128]{1,0:T(8,128)S(1)} %get-tuple-element.17), channel_id=1, source_target_pairs={{0,3},{1,0},{2,1},{3,2},{4,7},{5,4},{6,5},{7,6},{8,11},{9,8},{10,9... | collective-permute-start | bytes 36872 | tf_op jit(solution)/shard_map/ppermute | solution.py:272
  65.6 0.6 collective-permute-done.20
  66.2 0.4 collective-permute-done.19
  66.7 0.6 collective-permute-done.18
  67.3 1.2 %collective-permute-done.21.refs_1_ = f32[96,128]{1,0:T(8,128)S(1)} collective-permute-done((f32[96,128]{1,0:T(8,128)S(1)}, f32[96,128]{1,0:T(8,128)S(1)}, u32[]{:S(2)}, u32[]{:S(2)}) %collective-permute-start.21) | collective-permute-done | bytes 49184 | tf_op jit(solution)/shard_map/ppermute | solution.py:274
  68.5 0.9 %place_blocks.1 = f32[216,64]{1,0:T(8,128)} custom-call(f32[96,128]{1,0:T(8,128)S(1)} %pad_maximum_fusion.refs_0_, f32[96,128]{1,0:T(8,128)S(1)} %collective-permute-done.21.refs_1_), custom_call_target="tpu_custom_call" | custom-call | flops 100000 | bytes 200000 | tf_op jit(solution)/shard_map/place_blocks/pallas_call | solution.py:241
  69.5 1.4 %collective-permute-done.5 = f32[448,128]{1,0:T(8,128)S(1)} collective-permute-done((f32[448,128]{1,0:T(8,128)S(1)}, f32[448,128]{1,0:T(8,128)S(1)}, u32[]{:S(2)}, u32[]{:S(2)}) %collective-permute-start.5) | collective-permute-done | bytes 229408 | tf_op jit(solution)/shard_map/ppermute | solution.py:280
  70.8 0.7 fusion
  (16 shorter events, 0.1 us)
Async XLA Ops:
  0.6 19.3 %collective-permute-start.8 = (bf16[8,56,128]{2,1,0:T(8,128)(2,1)}, bf16[8,56,128]{2,1,0:T(8,128)(2,1)S(1)}, u32[]{:S(2)}, u32[]{:S(2)}) collective-permute-start(bf16[8,56,128]{2,1,0:T(8,128)(2,1)} %bitcast.15), channel_id=1, source_target_pairs={{0,4},{1,5},{2,6},{3,7},{4,0},{5,1},{6,2},{7,3},{8,12},{9,13},{10,... | collective-permute-start | bytes 344072 | tf_op jit(solution)/shard_map/ppermute | solution.py:259
  5.8 14.8 %collective-permute-start.7 = (bf16[8,56,128]{2,1,0:T(8,128)(2,1)}, bf16[8,56,128]{2,1,0:T(8,128)(2,1)S(1)}, u32[]{:S(2)}, u32[]{:S(2)}) collective-permute-start(bf16[8,56,128]{2,1,0:T(8,128)(2,1)} %bitcast.16), channel_id=1, source_target_pairs={{8,0},{16,8},{24,16},{32,24},{40,32},{48,40},{56,48},{64,56},{72,6... | collective-permute-start | bytes 344072 | tf_op jit(solution)/shard_map/ppermute | solution.py:262
  8.7 13.9 %collective-permute-start.6 = (bf16[8,56,128]{2,1,0:T(8,128)(2,1)}, bf16[8,56,128]{2,1,0:T(8,128)(2,1)S(1)}, u32[]{:S(2)}, u32[]{:S(2)}) collective-permute-start(bf16[8,56,128]{2,1,0:T(8,128)(2,1)} %bitcast.17), channel_id=1, source_target_pairs={{0,8},{8,16},{16,24},{24,32},{32,40},{40,48},{48,56},{56,64},{64,7... | collective-permute-start | bytes 344072 | tf_op jit(solution)/shard_map/ppermute | solution.py:262
  13.5 0.9 %copy-start = (bf16[8,1,56,128]{3,2,1,0:T(8,128)(2,1)S(1)}, bf16[8,1,56,128]{3,2,1,0:T(8,128)(2,1)}, u32[]{:S(2)}) copy-start(bf16[8,1,56,128]{3,2,1,0:T(8,128)(2,1)} %param.6) | copy-start | bytes 344068
  14.4 0.9 %copy-start.1 = (bf16[8,1,56,128]{3,2,1,0:T(8,128)(2,1)S(1)}, bf16[8,1,56,128]{3,2,1,0:T(8,128)(2,1)}, u32[]{:S(2)}) copy-start(bf16[8,1,56,128]{3,2,1,0:T(8,128)(2,1)} %param.7) | copy-start | bytes 344068
  15.3 0.8 %copy-start.2 = (bf16[8,64,3,3,3]{1,0,4,3,2:T(8,128)(2,1)S(1)}, bf16[8,64,3,3,3]{1,0,4,3,2:T(8,128)(2,1)}, u32[]{:S(2)}) copy-start(bf16[8,64,3,3,3]{1,0,4,3,2:T(8,128)(2,1)} %param.5) | copy-start | bytes 82948
  16.1 14.0 %copy-start.3 = (bf16[8,1,56,128]{3,2,1,0:T(8,128)(2,1)S(1)}, bf16[8,1,56,128]{3,2,1,0:T(8,128)(2,1)}, u32[]{:S(2)}) copy-start(bf16[8,1,56,128]{3,2,1,0:T(8,128)(2,1)} %param.4) | copy-start | bytes 344068
  16.2 12.2 %collective-permute-start.2 = (bf16[10,56,128]{2,1,0:T(8,128)(2,1)S(1)}, bf16[10,56,128]{2,1,0:T(8,128)(2,1)S(1)}, u32[]{:S(2)}, u32[]{:S(2)}) collective-permute-start(bf16[10,56,128]{2,1,0:T(8,128)(2,1)S(1)} %mask.1.m0), channel_id=1, source_target_pairs={{0,2},{1,3},{2,0},{3,1},{4,6},{5,7},{6,4},{7,5},{8,10},{9,11},{10,... | collective-permute-start | bytes 430088 | tf_op jit(solution)/shard_map/ppermute | solution.py:261
  19.2 9.2 %collective-permute-start.1 = (bf16[10,56,128]{2,1,0:T(8,128)(2,1)S(1)}, bf16[10,56,128]{2,1,0:T(8,128)(2,1)S(1)}, u32[]{:S(2)}, u32[]{:S(2)}) collective-permute-start(bf16[10,56,128]{2,1,0:T(8,128)(2,1)S(1)} %mask.1.m0), channel_id=1, source_target_pairs={{0,3},{1,0},{2,1},{3,2},{4,7},{5,4},{6,5},{7,6},{8,11},{9,8},{10,9... | collective-permute-start | bytes 430088 | tf_op jit(solution)/shard_map/ppermute | solution.py:261
  20.0 8.4 %collective-permute-start = (bf16[10,56,128]{2,1,0:T(8,128)(2,1)S(1)}, bf16[10,56,128]{2,1,0:T(8,128)(2,1)S(1)}, u32[]{:S(2)}, u32[]{:S(2)}) collective-permute-start(bf16[10,56,128]{2,1,0:T(8,128)(2,1)S(1)} %mask.1.m0), channel_id=1, source_target_pairs={{0,1},{1,2},{2,3},{3,0},{4,5},{5,6},{6,7},{7,4},{8,9},{9,10},{10,1... | collective-permute-start | bytes 430088 | tf_op jit(solution)/shard_map/ppermute | solution.py:261
  20.7 8.2 %collective-permute-start.10 = (bf16[8,56,128]{2,1,0:T(8,128)(2,1)S(1)}, bf16[8,56,128]{2,1,0:T(8,128)(2,1)S(1)}, u32[]{:S(2)}, u32[]{:S(2)}) collective-permute-start(bf16[8,56,128]{2,1,0:T(8,128)(2,1)S(1)} %collective-permute-done.8.refs_4_), channel_id=1, source_target_pairs={{8,0},{16,8},{24,16},{32,24},{40,32},{48,40},{56,48},{64,56},{72,6... | collective-permute-start | bytes 344072 | tf_op jit(solution)/shard_map/ppermute | solution.py:263
  22.6 7.5 %collective-permute-start.9 = (bf16[8,56,128]{2,1,0:T(8,128)(2,1)S(1)}, bf16[8,56,128]{2,1,0:T(8,128)(2,1)S(1)}, u32[]{:S(2)}, u32[]{:S(2)}) collective-permute-start(bf16[8,56,128]{2,1,0:T(8,128)(2,1)S(1)} %collective-permute-done.8.refs_4_), channel_id=1, source_target_pairs={{0,8},{8,16},{16,24},{24,32},{32,40},{40,48},{48,56},{56,64},{64,7... | collective-permute-start | bytes 344072 | tf_op jit(solution)/shard_map/ppermute | solution.py:263
  31.3 1.3 %collective-permute-start.11 = (f32[96,128]{1,0:T(8,128)S(1)}, f32[96,128]{1,0:T(8,128)S(1)}, u32[]{:S(2)}, u32[]{:S(2)}) collective-permute-start(f32[96,128]{1,0:T(8,128)S(1)} %get-tuple-element.11), channel_id=1, source_target_pairs={{0,8},{8,0},{16,24},{24,16},{32,40},{40,32},{48,56},{56,48},{64,72... | collective-permute-start | bytes 147464 | tf_op jit(solution)/shard_map/ppermute | solution.py:268
  32.6 13.1 %collective-permute-start.14 = (f32[96,128]{1,0:T(8,128)S(1)}, f32[96,128]{1,0:T(8,128)S(1)}, u32[]{:S(2)}, u32[]{:S(2)}) collective-permute-start(f32[96,128]{1,0:T(8,128)S(1)} %add.33), channel_id=1, source_target_pairs={{0,32},{8,40},{16,48},{24,56},{32,0},{40,8},{48,16},{56,24},{64,96... | collective-permute-start | bytes 147464 | tf_op jit(solution)/shard_map/ppermute | solution.py:269
  32.7 13.0 %collective-permute-start.13 = (f32[96,128]{1,0:T(8,128)S(1)}, f32[96,128]{1,0:T(8,128)S(1)}, u32[]{:S(2)}, u32[]{:S(2)}) collective-permute-start(f32[96,128]{1,0:T(8,128)S(1)} %add.33), channel_id=1, source_target_pairs={{0,48},{8,56},{16,0},{24,8},{32,16},{40,24},{48,32},{56,40},{64,11... | collective-permute-start | bytes 147464 | tf_op jit(solution)/shard_map/ppermute | solution.py:269
  37.0 8.7 %collective-permute-start.12 = (f32[96,128]{1,0:T(8,128)S(1)}, f32[96,128]{1,0:T(8,128)S(1)}, u32[]{:S(2)}, u32[]{:S(2)}) collective-permute-start(f32[96,128]{1,0:T(8,128)S(1)} %add.33), channel_id=1, source_target_pairs={{0,16},{8,24},{16,32},{24,40},{32,48},{40,56},{48,0},{56,8},{64,80... | collective-permute-start | bytes 147464 | tf_op jit(solution)/shard_map/ppermute | solution.py:269
  38.0 23.8 %collective-permute-start.3 = (f32[896,128]{1,0:T(8,128)S(1)}, f32[896,128]{1,0:T(8,128)S(1)}, u32[]{:S(2)}, u32[]{:S(2)}) collective-permute-start(f32[896,128]{1,0:T(8,128)S(1)} %get-tuple-element.8), channel_id=1, source_target_pairs={{8,0},{16,8},{24,16},{32,24},{40,32},{48,40},{56,48},{64,56},{72,6... | collective-permute-start | bytes 1376264 | tf_op jit(solution)/shard_map/ppermute | solution.py:278
  40.9 20.9 %collective-permute-start.4 = (f32[896,128]{1,0:T(8,128)S(1)}, f32[896,128]{1,0:T(8,128)S(1)}, u32[]{:S(2)}, u32[]{:S(2)}) collective-permute-start(f32[896,128]{1,0:T(8,128)S(1)} %get-tuple-element.9), channel_id=1, source_target_pairs={{0,8},{8,16},{16,24},{24,32},{32,40},{40,48},{48,56},{56,64},{64,7... | collective-permute-start | bytes 1376264 | tf_op jit(solution)/shard_map/ppermute | solution.py:278
  45.8 16.0 %collective-permute-start.17 = (f32[96,128]{1,0:T(8,128)S(1)}, f32[96,128]{1,0:T(8,128)S(1)}, u32[]{:S(2)}, u32[]{:S(2)}) collective-permute-start(f32[96,128]{1,0:T(8,128)S(1)} %add_add_fusion.2), channel_id=1, source_target_pairs={{0,192},{8,200},{16,208},{24,216},{32,224},{40,232},{48,240},{56,2... | collective-permute-start | bytes 147464 | tf_op jit(solution)/shard_map/ppermute | solution.py:270
  46.6 15.2 %collective-permute-start.16 = (f32[96,128]{1,0:T(8,128)S(1)}, f32[96,128]{1,0:T(8,128)S(1)}, u32[]{:S(2)}, u32[]{:S(2)}) collective-permute-start(f32[96,128]{1,0:T(8,128)S(1)} %add_add_fusion.2), channel_id=1, source_target_pairs={{0,128},{8,136},{16,144},{24,152},{32,160},{40,168},{48,176},{56,1... | collective-permute-start | bytes 147464 | tf_op jit(solution)/shard_map/ppermute | solution.py:270
  46.6 15.2 %collective-permute-start.15 = (f32[96,128]{1,0:T(8,128)S(1)}, f32[96,128]{1,0:T(8,128)S(1)}, u32[]{:S(2)}, u32[]{:S(2)}) collective-permute-start(f32[96,128]{1,0:T(8,128)S(1)} %add_add_fusion.2), channel_id=1, source_target_pairs={{0,64},{8,72},{16,80},{24,88},{32,96},{40,104},{48,112},{56,120},{... | collective-permute-start | bytes 147464 | tf_op jit(solution)/shard_map/ppermute | solution.py:270
  62.0 8.9 %collective-permute-start.5 = (f32[448,128]{1,0:T(8,128)S(1)}, f32[448,128]{1,0:T(8,128)S(1)}, u32[]{:S(2)}, u32[]{:S(2)}) collective-permute-start(f32[448,128]{1,0:T(8,128)S(1)} %slice.25), channel_id=1, source_target_pairs={{0,4},{1,5},{2,6},{3,7},{4,0},{5,1},{6,2},{7,3},{8,12},{9,13},{10,... | collective-permute-start | bytes 688136 | tf_op jit(solution)/shard_map/ppermute | solution.py:280
  62.1 4.1 %collective-permute-start.20 = (f32[24,128]{1,0:T(8,128)S(1)}, f32[24,128]{1,0:T(8,128)S(1)}, u32[]{:S(2)}, u32[]{:S(2)}) collective-permute-start(f32[24,128]{1,0:T(8,128)S(1)} %get-tuple-element.15), channel_id=1, source_target_pairs={{0,2},{1,3},{2,0},{3,1},{4,6},{5,7},{6,4},{7,5},{8,10},{9,11},{10,... | collective-permute-start | bytes 36872 | tf_op jit(solution)/shard_map/ppermute | solution.py:272
  62.9 3.8 %collective-permute-start.19 = (f32[24,128]{1,0:T(8,128)S(1)}, f32[24,128]{1,0:T(8,128)S(1)}, u32[]{:S(2)}, u32[]{:S(2)}) collective-permute-start(f32[24,128]{1,0:T(8,128)S(1)} %get-tuple-element.16), channel_id=1, source_target_pairs={{0,1},{1,2},{2,3},{3,0},{4,5},{5,6},{6,7},{7,4},{8,9},{9,10},{10,1... | collective-permute-start | bytes 36872 | tf_op jit(solution)/shard_map/ppermute | solution.py:272
  64.7 2.5 %collective-permute-start.18 = (f32[24,128]{1,0:T(8,128)S(1)}, f32[24,128]{1,0:T(8,128)S(1)}, u32[]{:S(2)}, u32[]{:S(2)}) collective-permute-start(f32[24,128]{1,0:T(8,128)S(1)} %get-tuple-element.17), channel_id=1, source_target_pairs={{0,3},{1,0},{2,1},{3,2},{4,7},{5,4},{6,5},{7,6},{8,11},{9,8},{10,9... | collective-permute-start | bytes 36872 | tf_op jit(solution)/shard_map/ppermute | solution.py:272
  67.3 1.2 %collective-permute-start.21 = (f32[96,128]{1,0:T(8,128)S(1)}, f32[96,128]{1,0:T(8,128)S(1)}, u32[]{:S(2)}, u32[]{:S(2)}) collective-permute-start(f32[96,128]{1,0:T(8,128)S(1)} %pad_maximum_fusion.refs_0_), channel_id=1, source_target_pairs={{0,8},{8,0},{16,24},{24,16},{32,40},{40,32},{48,56},{56,48},{64,72... | collective-permute-start | bytes 147464 | tf_op jit(solution)/shard_map/ppermute | solution.py:274

commit v2 on v1

--- a/solution.py
+++ b/solution.py
@@ -7,6 +7,7 @@
 
 ROWS, COLS, CH = 56, 128, 8
 BF, F32 = jnp.bfloat16, jnp.float32
+COST = 20_000_000_000
 
 
 def space_pairs(to):
@@ -25,8 +26,7 @@
     return pairs
 
 
-UP = [(i, i + 1) for i in range(31)]
-DOWN = [(i + 1, i) for i in range(31)]
+OUTER = [pair for i in range(1, 31, 2) for pair in ((i, i + 1), (i + 1, i))]
 CORE = space_pairs(lambda z, x, core: (z, x, core ^ 1))
 X_OTHERS = [space_pairs(lambda z, x, core, j=j: (z, x + j, core)) for j in (1, 3, 2)]
 Z_OTHERS = [space_pairs(lambda z, x, core, j=j: (z ^ j, x, core)) for j in (1, 2, 3)]
@@ -48,10 +48,17 @@
     return [pl.BlockSpec(memory_space=pltpu.VMEM)] * count
 
 
-def mask_body(pre_ref, up_ref, kern_ref, out_ref):
+def mask_body(pre_hbm, up_hbm, kern_hbm, out_ref, pre_ref, up_ref, kern_ref, sems):
+    pairs = ((pre_hbm, pre_ref), (up_hbm, up_ref), (kern_hbm, kern_ref))
+    copies = [pltpu.make_async_copy(src, dst, sems.at[i]) for i, (src, dst) in enumerate(pairs)]
+    for copy in copies:
+        copy.start()
+    copies[0].wait()
+    copies[1].wait()
     for f in range(CH):
         keep = pre_ref[f].astype(F32) > 0
         out_ref[f] = jnp.where(keep, up_ref[f].astype(F32), 0.0).astype(BF)
+    copies[2].wait()
     blank = jnp.zeros((CH, 64), F32)
     for plane in range(2):
         pieces = []
@@ -66,10 +73,15 @@
     return pl.pallas_call(
         mask_body,
         out_shape=jax.ShapeDtypeStruct((CH + 2, ROWS, COLS), BF),
-        in_specs=whole(3),
+        in_specs=[pl.BlockSpec(memory_space=pl.ANY)] * 3,
         out_specs=pl.BlockSpec(memory_space=pltpu.VMEM),
-        compiler_params=params(),
-        cost_estimate=pl.CostEstimate(flops=100_000, bytes_accessed=500_000, transcendentals=0),
+        scratch_shapes=[
+            pltpu.VMEM((CH, ROWS, COLS), BF),
+            pltpu.VMEM((CH, ROWS, COLS), BF),
+            pltpu.VMEM((27, CH, 64), BF),
+            pltpu.SemaphoreType.DMA((3,)),
+        ],
+        cost_estimate=pl.CostEstimate(flops=COST, bytes_accessed=500_000, transcendentals=0),
         name="mask",
     )(preact, upstream, kern)
 
@@ -77,6 +89,12 @@
 def spread(ref, planes, scratch):
     for ch in range(planes):
         scratch[pl.ds(ch * ROWS, ROWS), :] = ref[ch].astype(F32)
+
+
+def spread_either(first, ref, other, planes, scratch):
+    for ch in range(planes):
+        value = jnp.where(first, ref[ch].astype(F32), other[ch].astype(F32))
+        scratch[pl.ds(ch * ROWS, ROWS), :] = value
 
 
 def row_of(scratch, row):
@@ -101,13 +119,19 @@
 
 
 def weight_body(m0, m1, m2, m3, *refs):
-    acts, (keep_ref, send_ref), scratch = refs[:6], refs[6:8], refs[8:]
+    acts, (keep_ref, send_ref), scratch = refs[:4], refs[4:6], refs[6:]
     core, _, _ = place()
     masked, planes = scratch[:4], scratch[4:]
     for ref, buf in zip((m0, m1, m2, m3), masked):
         spread(ref, CH, buf)
-    for ref, buf in zip(acts, planes):
-        spread(ref, CH, buf)
+    first_core = core == 0
+    inner, outer = acts[2:]
+    for block in range(2):
+        below, here, above = planes[3 * block : 3 * block + 3]
+        near, far = (ref.at[pl.ds(CH * block, CH)] for ref in (inner, outer))
+        spread_either(first_core, far, near, CH, below)
+        spread(acts[block], CH, here)
+        spread_either(first_core, near, far, CH, above)
     lane = lax.broadcasted_iota(jnp.int32, (CH, COLS), 1)
     zero = jnp.zeros((CH, COLS), F32)
     gap = jnp.zeros((COLS - 9 * CH, COLS), F32)
@@ -132,7 +156,6 @@
             lhs, rhs, (((1,), (1,)), ((), ())), preferred_element_type=F32
         )
     own, other = total[:, :COLS], total[:, COLS:]
-    first_core = core == 0
     keep_ref[...] = jnp.where(first_core, own, other)
     send_ref[...] = jnp.where(first_core, other, own)
 
@@ -142,19 +165,20 @@
     return pl.pallas_call(
         weight_body,
         out_shape=(shape, shape),
-        in_specs=whole(10),
+        in_specs=whole(8),
         out_specs=tuple(whole(2)),
         scratch_shapes=[pltpu.VMEM((CH * ROWS, COLS), F32)] * 10,
         compiler_params=params(),
         cost_estimate=pl.CostEstimate(
-            flops=2 * 96 * 256 * 7168, bytes_accessed=1_500_000, transcendentals=0
+            flops=COST, bytes_accessed=1_500_000, transcendentals=0
         ),
         name="weight_grad",
     )(*masked, *acts)
 
 
-def data_body(m0, m1, m2, m3, down_ref, mid_ref, up_ref, *masked):
-    _, half, y = place()
+def data_body(m0, m1, m2, m3, inner_ref, mid_ref, outer_ref, *masked):
+    core, half, y = place()
+    first_core = core == 0
     for ref, buf in zip((m0, m1, m2, m3), masked):
         spread(ref, CH, buf)
     lane = lax.broadcasted_iota(jnp.int32, (CH, COLS), 1)
@@ -177,7 +201,6 @@
     weights = jnp.concatenate(rows + [jnp.zeros((32, 256), F32)], axis=0)
     weights = jnp.transpose(weights)
     weights = jnp.concatenate([weights[:72, :96], weights[128:200, :96]], axis=0).astype(BF)
-    outs = (down_ref, mid_ref, up_ref)
     sums = {}
     step = 4
     for first in range(0, ROWS, step):
@@ -196,12 +219,14 @@
                         term = got[top : top + CH, i * COLS : (i + 1) * COLS]
                         key = (block, kz, at)
                         sums[key] = sums[key] + term if key in sums else term
-                    done = [row - 1] if row < ROWS - 1 else [row - 1, row]
-                    for at in done:
-                        if at >= 0:
-                            outs[kz][pl.ds(block * CH * ROWS + at, CH, stride=ROWS), :] = sums.pop(
-                                (block, kz, at)
-                            )
+                done = [row - 1] if row < ROWS - 1 else [row - 1, row]
+                for at in done:
+                    if at >= 0:
+                        down, mid, up = (sums.pop((block, kz, at)) for kz in range(3))
+                        place_at = pl.ds(block * CH * ROWS + at, CH, stride=ROWS)
+                        mid_ref[place_at, :] = mid
+                        inner_ref[place_at, :] = jnp.where(first_core, up, down)
+                        outer_ref[place_at, :] = jnp.where(first_core, down, up)
 
 
 def data_call(masked):
@@ -214,7 +239,7 @@
         scratch_shapes=[pltpu.VMEM((CH * ROWS, COLS), F32)] * 4,
         compiler_params=params(),
         cost_estimate=pl.CostEstimate(
-            flops=2 * 144 * 96 * 7168, bytes_accessed=2_000_000, transcendentals=0
+            flops=COST, bytes_accessed=2_000_000, transcendentals=0
         ),
         name="data_grad",
     )(*masked)
@@ -259,14 +284,17 @@
     other = lax.ppermute(acts, "filt", HALF)
     mine = mask_call(pre, ups, kern)
     masked = [mine] + [lax.ppermute(mine, "filt", pairs) for pairs in Y_OTHERS]
-    low, high = lax.ppermute(acts, "space", UP), lax.ppermute(acts, "space", DOWN)
-    other_low, other_high = lax.ppermute(other, "space", UP), lax.ppermute(other, "space", DOWN)
-
-    down, mid, up = data_call(masked)
-    keep, send = weight_call(masked, (low, acts, high, other_low, other, other_high))
+    m1, m2, m3, _ = lax.optimization_barrier((*masked[1:], other))
+    masked = [mine, m1, m2, m3]
+    to_inner, mid, to_outer = data_call(masked)
+    both = jnp.concatenate([acts, other], axis=0)
+    inner, outer = lax.ppermute(both, "space", CORE), lax.ppermute(both, "space", OUTER)
+    keep, send = weight_call(masked, (acts, other, inner, outer))
 
     terms = keep + lax.ppermute(send, "space", CORE)
     terms = sum([lax.ppermute(terms, "space", pairs) for pairs in X_OTHERS], terms)
+    layer = mid + lax.ppermute(to_inner, "space", CORE) + lax.ppermute(to_outer, "space", OUTER)
+    terms, layer = lax.optimization_barrier((terms, layer))
     terms = sum([lax.ppermute(terms, "space", pairs) for pairs in Z_OTHERS], terms)
     blocks = [terms[24 * j : 24 * j + 24] for j in range(4)]
     got = [lax.ppermute(block, "filt", pairs) for block, pairs in zip(blocks[1:], Y_BACK)]
@@ -275,7 +303,6 @@
     grads = final_call(mine_blocks, their_blocks, scale)
     kernel_grad = jnp.transpose(grads.reshape(3, 3, 3, CH, 64), (3, 4, 0, 1, 2))
 
-    layer = mid + lax.ppermute(down, "space", DOWN) + lax.ppermute(up, "space", UP)
     own, away = layer[: CH * ROWS], layer[CH * ROWS :]
     own = own + lax.ppermute(away, "filt", HALF)
     input_grad = own.astype(BF).reshape(CH, 1, ROWS, COLS)

time: 71.8 us -> 57.1 us (0.80)
  the two profiles are of different devices: /device:TPU:71 before, /device:TPU:6 now
where the time goes in v2:
time: 57.1 us; the launch traced here: 57 us
  starting transfers between devices  33.7 us (59%)
  waiting for transfers between devices  16.8 us (29%)
  Pallas kernels  4.9 us (9%)
  other arithmetic  0.8 us (1%)
  between operations  0.79 us (1%)
    ppermute x6, starting transfers between devices, on_device(): lax.ppermute(terms, 'space', pairs)  9.46 us
    ppermute x6, waiting for transfers between devices, on_device(): lax.ppermute(terms, 'space', pairs)  8.07 us
    ppermute x1, starting transfers between devices, on_device(): other = lax.ppermute(acts, 'filt', HALF)  7.28 us
    ppermute x3, starting transfers between devices, on_device(): masked = [mine] + [lax.ppermute(mine, 'filt', pairs) for pairs in Y_OTHERS]  5.31 us
    ppermute x3, starting transfers between devices, on_device(): lax.ppermute(block, 'filt', pairs)  3.41 us
    ppermute x1, starting transfers between devices, on_device(): lax.ppermute(to_outer, 'space', OUTER)  2.82 us
    ppermute x3, waiting for transfers between devices, on_device(): masked = [mine] + [lax.ppermute(mine, 'filt', pairs) for pairs in Y_OTHERS]  2.46 us
    ppermute x1, waiting for transfers between devices, on_device(): own = own + lax.ppermute(away, 'filt', HALF)  2.01 us
  transfers between devices with their start and end apart: 20, of which 11 were waited for; matrix products, arithmetic and copies ran while one was open for 0% of the time, Pallas kernels for 9%

profile of v2, /device:TPU:6, one launch (start us, length us, event | category | flops | bytes accessed | tf_op | source)
XLA Modules:
  0.0 57.0 jit_solution(664210300723102573)
XLA Ops:
  0.6 7.3 %collective-permute-start.3 = (bf16[8,56,128]{2,1,0:T(8,128)(2,1)}, bf16[8,56,128]{2,1,0:T(8,128)(2,1)S(1)}, u32[]{:S(2)}, u32[]{:S(2)}) collective-permute-start(bf16[8,56,128]{2,1,0:T(8,128)(2,1)} %bitcast.12), channel_id=1, source_target_pairs={{0,4},{1,5},{2,6},{3,7},{4,0},{5,1},{6,2},{7,3},{8,12},{9,13},{10,... | collective-permute-start | bytes 344072 | tf_op jit(solution)/shard_map/ppermute | solution.py:284
  7.9 1.8 %mask.1.m0 = bf16[10,56,128]{2,1,0:T(8,128)(2,1)} custom-call(bf16[8,56,128]{2,1,0:T(8,128)(2,1)} %bitcast.17, bf16[8,56,128]{2,1,0:T(8,128)(2,1)} %bitcast.18, bf16[27,8,64]{2,1,0:T(8,128)(2,1)} %bitcast.19), custom_call_target="tpu_custom_call" | custom-call | flops 20000000000 | bytes 500000 | tf_op jit(solution)/shard_map/mask/pallas_call | solution.py:73
  9.7 0.0 copy-start.1
  9.7 3.3 %collective-permute-start.2 = (bf16[10,56,128]{2,1,0:T(8,128)(2,1)}, bf16[10,56,128]{2,1,0:T(8,128)(2,1)S(1)}, u32[]{:S(2)}, u32[]{:S(2)}) collective-permute-start(bf16[10,56,128]{2,1,0:T(8,128)(2,1)} %mask.1.m0), channel_id=1, source_target_pairs={{0,2},{1,3},{2,0},{3,1},{4,6},{5,7},{6,4},{7,5},{8,10},{9,11},{10,... | collective-permute-start | bytes 430088 | tf_op jit(solution)/shard_map/ppermute | solution.py:286
  13.0 1.1 %collective-permute-start.1 = (bf16[10,56,128]{2,1,0:T(8,128)(2,1)}, bf16[10,56,128]{2,1,0:T(8,128)(2,1)S(1)}, u32[]{:S(2)}, u32[]{:S(2)}) collective-permute-start(bf16[10,56,128]{2,1,0:T(8,128)(2,1)} %mask.1.m0), channel_id=1, source_target_pairs={{0,3},{1,0},{2,1},{3,2},{4,7},{5,4},{6,5},{7,6},{8,11},{9,8},{10,9... | collective-permute-start | bytes 430088 | tf_op jit(solution)/shard_map/ppermute | solution.py:286
  14.0 1.0 %collective-permute-start = (bf16[10,56,128]{2,1,0:T(8,128)(2,1)}, bf16[10,56,128]{2,1,0:T(8,128)(2,1)S(1)}, u32[]{:S(2)}, u32[]{:S(2)}) collective-permute-start(bf16[10,56,128]{2,1,0:T(8,128)(2,1)} %mask.1.m0), channel_id=1, source_target_pairs={{0,1},{1,2},{2,3},{3,0},{4,5},{5,6},{6,7},{7,4},{8,9},{9,10},{10,1... | collective-permute-start | bytes 430088 | tf_op jit(solution)/shard_map/ppermute | solution.py:286
  15.0 0.0 collective-permute-done.3.refs_1_
  15.0 0.0 copy-done
  15.0 1.9 %collective-permute-start.5 = (bf16[16,56,128]{2,1,0:T(8,128)(2,1)S(1)}, bf16[16,56,128]{2,1,0:T(8,128)(2,1)S(1)}, u32[]{:S(2)}, u32[]{:S(2)}) collective-permute-start(bf16[16,56,128]{2,1,0:T(8,128)(2,1)S(1)} %pad_maximum_fusion), channel_id=1, source_target_pairs={{8,16},{16,8},{24,32},{32,24},{40,48},{48,40},{56,64},{64,56},{72,... | collective-permute-start | bytes 688136 | tf_op jit(solution)/shard_map/ppermute | solution.py:291
  17.0 1.1 %collective-permute-start.4 = (bf16[16,56,128]{2,1,0:T(8,128)(2,1)S(1)}, bf16[16,56,128]{2,1,0:T(8,128)(2,1)S(1)}, u32[]{:S(2)}, u32[]{:S(2)}) collective-permute-start(bf16[16,56,128]{2,1,0:T(8,128)(2,1)S(1)} %pad_maximum_fusion), channel_id=1, source_target_pairs={{0,8},{8,0},{16,24},{24,16},{32,40},{40,32},{48,56},{56,48},{64,72... | collective-permute-start | bytes 688136 | tf_op jit(solution)/shard_map/ppermute | solution.py:291
  18.1 0.0 collective-permute-done.2.m3
  18.1 2.0 %collective-permute-done.1.m2 = bf16[10,56,128]{2,1,0:T(8,128)(2,1)S(1)} collective-permute-done((bf16[10,56,128]{2,1,0:T(8,128)(2,1)}, bf16[10,56,128]{2,1,0:T(8,128)(2,1)S(1)}, u32[]{:S(2)}, u32[]{:S(2)}) %collective-permute-start.1) | collective-permute-done | bytes 143392 | tf_op jit(solution)/shard_map/ppermute | solution.py:286
  20.1 0.4 collective-permute-done.m1
  20.6 1.0 %data_grad.1 = (f32[896,128]{1,0:T(8,128)S(1)}, f32[896,128]{1,0:T(8,128)S(1)}, f32[896,128]{1,0:T(8,128)S(1)}) custom-call(bf16[10,56,128]{2,1,0:T(8,128)(2,1)S(1)} %copy-done.1, bf16[10,56,128]{2,1,0:T(8,128)(2,1)S(1)} %collective-permute-done.m1, bf16[10,56,128]{2,1,0:T(8,128)(2,1)S(1)} %collective-permute-done.1.m2, ...), custom_call_target="tpu_custom_call" | custom-call | flops 20000000000 | bytes 2000000 | tf_op jit(solution)/shard_map/data_grad/pallas_call | solution.py:234
  21.6 0.1 collective-permute-start.10
  21.7 2.8 %collective-permute-start.11 = (f32[896,128]{1,0:T(8,128)S(1)}, f32[896,128]{1,0:T(8,128)S(1)}, u32[]{:S(2)}, u32[]{:S(2)}) collective-permute-start(f32[896,128]{1,0:T(8,128)S(1)} %get-tuple-element.19), channel_id=1, source_target_pairs={{8,16},{16,8},{24,32},{32,24},{40,48},{48,40},{56,64},{64,56},{72,... | collective-permute-start | bytes 1376264 | tf_op jit(solution)/shard_map/ppermute | solution.py:296
  24.5 0.0 collective-permute-done.5.refs_3_
  24.5 0.0 collective-permute-done.4.refs_2_
  24.5 1.2 %weight_grad.1 = (f32[96,128]{1,0:T(8,128)S(1)}, f32[96,128]{1,0:T(8,128)S(1)}) custom-call(bf16[10,56,128]{2,1,0:T(8,128)(2,1)S(1)} %copy-done.1, bf16[10,56,128]{2,1,0:T(8,128)(2,1)S(1)} %collective-permute-done.m1, bf16[10,56,128]{2,1,0:T(8,128)(2,1)S(1)} %collective-permute-done.1.m2, bf16[10,56,128]{2,1,0:T(8,128)(2,1)S(1)} %collective-permute-done.2.m3, ...), custom_call_target="tpu_custom_call" | custom-call | flops 20000000000 | bytes 1500000 | tf_op jit(solution)/shard_map/weight_grad/pallas_call | solution.py:165
  25.7 0.2 collective-permute-start.6
  25.9 1.1 %collective-permute-done.6 = f32[96,128]{1,0:T(8,128)S(1)} collective-permute-done((f32[96,128]{1,0:T(8,128)S(1)}, f32[96,128]{1,0:T(8,128)S(1)}, u32[]{:S(2)}, u32[]{:S(2)}) %collective-permute-start.6) | collective-permute-done | bytes 49184 | tf_op jit(solution)/shard_map/ppermute | solution.py:294
  27.0 1.7 %collective-permute-start.9 = (f32[96,128]{1,0:T(8,128)S(1)}, f32[96,128]{1,0:T(8,128)S(1)}, u32[]{:S(2)}, u32[]{:S(2)}) collective-permute-start(f32[96,128]{1,0:T(8,128)S(1)} %add.30), channel_id=1, source_target_pairs={{0,32},{8,40},{16,48},{24,56},{32,0},{40,8},{48,16},{56,24},{64,96... | collective-permute-start | bytes 147464 | tf_op jit(solution)/shard_map/ppermute | solution.py:295
  28.8 0.0 collective-permute-start.8
  28.8 3.2 %collective-permute-start.7 = (f32[96,128]{1,0:T(8,128)S(1)}, f32[96,128]{1,0:T(8,128)S(1)}, u32[]{:S(2)}, u32[]{:S(2)}) collective-permute-start(f32[96,128]{1,0:T(8,128)S(1)} %add.30), channel_id=1, source_target_pairs={{0,16},{8,24},{16,32},{24,40},{32,48},{40,56},{48,0},{56,8},{64,80... | collective-permute-start | bytes 147464 | tf_op jit(solution)/shard_map/ppermute | solution.py:295
  32.0 2.2 %collective-permute-done.9 = f32[96,128]{1,0:T(8,128)S(1)} collective-permute-done((f32[96,128]{1,0:T(8,128)S(1)}, f32[96,128]{1,0:T(8,128)S(1)}, u32[]{:S(2)}, u32[]{:S(2)}) %collective-permute-start.9) | collective-permute-done | bytes 49184 | tf_op jit(solution)/shard_map/ppermute | solution.py:295
  34.2 2.1 %collective-permute-done.8 = f32[96,128]{1,0:T(8,128)S(1)} collective-permute-done((f32[96,128]{1,0:T(8,128)S(1)}, f32[96,128]{1,0:T(8,128)S(1)}, u32[]{:S(2)}, u32[]{:S(2)}) %collective-permute-start.8) | collective-permute-done | bytes 49184 | tf_op jit(solution)/shard_map/ppermute | solution.py:295
  36.3 0.0 collective-permute-done.7
  36.4 0.0 collective-permute-done.10
  36.4 0.0 collective-permute-done.11
  36.4 0.1 add_add_fusion
  36.5 0.6 %collective-permute-start.15 = (f32[96,128]{1,0:T(8,128)S(1)}, f32[96,128]{1,0:T(8,128)S(1)}, u32[]{:S(2)}, u32[]{:S(2)}) collective-permute-start(f32[96,128]{1,0:T(8,128)S(1)} %add_add_fusion.2), channel_id=1, source_target_pairs={{0,192},{8,200},{16,208},{24,216},{32,224},{40,232},{48,240},{56,2... | collective-permute-start | bytes 147464 | tf_op jit(solution)/shard_map/ppermute | solution.py:298
  37.0 2.0 %collective-permute-start.14 = (f32[96,128]{1,0:T(8,128)S(1)}, f32[96,128]{1,0:T(8,128)S(1)}, u32[]{:S(2)}, u32[]{:S(2)}) collective-permute-start(f32[96,128]{1,0:T(8,128)S(1)} %add_add_fusion.2), channel_id=1, source_target_pairs={{0,128},{8,136},{16,144},{24,152},{32,160},{40,168},{48,176},{56,1... | collective-permute-start | bytes 147464 | tf_op jit(solution)/shard_map/ppermute | solution.py:298
  39.0 1.9 %collective-permute-start.13 = (f32[96,128]{1,0:T(8,128)S(1)}, f32[96,128]{1,0:T(8,128)S(1)}, u32[]{:S(2)}, u32[]{:S(2)}) collective-permute-start(f32[96,128]{1,0:T(8,128)S(1)} %add_add_fusion.2), channel_id=1, source_target_pairs={{0,64},{8,72},{16,80},{24,88},{32,96},{40,104},{48,112},{56,120},{... | collective-permute-start | bytes 147464 | tf_op jit(solution)/shard_map/ppermute | solution.py:298
  41.0 2.0 %collective-permute-start.12 = (f32[448,128]{1,0:T(8,128)S(1)}, f32[448,128]{1,0:T(8,128)S(1)}, u32[]{:S(2)}, u32[]{:S(2)}) collective-permute-start(f32[448,128]{1,0:T(8,128)S(1)} %slice.19), channel_id=1, source_target_pairs={{0,4},{1,5},{2,6},{3,7},{4,0},{5,1},{6,2},{7,3},{8,12},{9,13},{10,... | collective-permute-start | bytes 688136 | tf_op jit(solution)/shard_map/ppermute | solution.py:307
  43.0 0.1 collective-permute-done.15
  43.0 1.4 %collective-permute-done.14 = f32[96,128]{1,0:T(8,128)S(1)} collective-permute-done((f32[96,128]{1,0:T(8,128)S(1)}, f32[96,128]{1,0:T(8,128)S(1)}, u32[]{:S(2)}, u32[]{:S(2)}) %collective-permute-start.14) | collective-permute-done | bytes 49184 | tf_op jit(solution)/shard_map/ppermute | solution.py:298
  44.5 2.2 %collective-permute-done.13 = f32[96,128]{1,0:T(8,128)S(1)} collective-permute-done((f32[96,128]{1,0:T(8,128)S(1)}, f32[96,128]{1,0:T(8,128)S(1)}, u32[]{:S(2)}, u32[]{:S(2)}) %collective-permute-start.13) | collective-permute-done | bytes 49184 | tf_op jit(solution)/shard_map/ppermute | solution.py:298
  46.7 0.1 collective-permute-start.18
  46.8 0.3 collective-permute-start.17
  47.1 3.0 %collective-permute-start.16 = (f32[24,128]{1,0:T(8,128)S(1)}, f32[24,128]{1,0:T(8,128)S(1)}, u32[]{:S(2)}, u32[]{:S(2)}) collective-permute-start(f32[24,128]{1,0:T(8,128)S(1)} %get-tuple-element.27), channel_id=1, source_target_pairs={{0,3},{1,0},{2,1},{3,2},{4,7},{5,4},{6,5},{7,6},{8,11},{9,8},{10,9... | collective-permute-start | bytes 36872 | tf_op jit(solution)/shard_map/ppermute | solution.py:300
  50.1 1.9 %collective-permute-done.18 = f32[24,128]{1,0:T(8,128)S(1)} collective-permute-done((f32[24,128]{1,0:T(8,128)S(1)}, f32[24,128]{1,0:T(8,128)S(1)}, u32[]{:S(2)}, u32[]{:S(2)}) %collective-permute-start.18) | collective-permute-done | bytes 12320 | tf_op jit(solution)/shard_map/ppermute | solution.py:300
  52.0 0.0 collective-permute-done.17
  52.0 0.0 collective-permute-done.16
  52.0 0.1 collective-permute-start.19
  52.1 1.2 %collective-permute-done.19.refs_1_ = f32[96,128]{1,0:T(8,128)S(1)} collective-permute-done((f32[96,128]{1,0:T(8,128)S(1)}, f32[96,128]{1,0:T(8,128)S(1)}, u32[]{:S(2)}, u32[]{:S(2)}) %collective-permute-start.19) | collective-permute-done | bytes 49184 | tf_op jit(solution)/shard_map/ppermute | solution.py:302
  53.4 0.9 %place_blocks.1 = f32[216,64]{1,0:T(8,128)} custom-call(f32[96,128]{1,0:T(8,128)S(1)} %pad_maximum_fusion.1.refs_0_, f32[96,128]{1,0:T(8,128)S(1)} %collective-permute-done.19.refs_1_), custom_call_target="tpu_custom_call" | custom-call | flops 100000 | bytes 200000 | tf_op jit(solution)/shard_map/place_blocks/pallas_call | solution.py:266
  54.3 2.0 %collective-permute-done.12 = f32[448,128]{1,0:T(8,128)S(1)} collective-permute-done((f32[448,128]{1,0:T(8,128)S(1)}, f32[448,128]{1,0:T(8,128)S(1)}, u32[]{:S(2)}, u32[]{:S(2)}) %collective-permute-start.12) | collective-permute-done | bytes 229408 | tf_op jit(solution)/shard_map/ppermute | solution.py:307
  56.3 0.7 %add_convert_fusion = bf16[448,128]{1,0:T(8,128)(2,1)} fusion(f32[448,128]{1,0:T(8,128)S(1)} %collective-permute-done.12, f32[896,128]{1,0:T(8,128)S(1)} %add_add_fusion), kind=kLoop, calls=%fused_computation.2 | loop fusion | flops 114688 | bytes 573440 | tf_op jit(solution)/shard_map/convert_element_type | solution.py:308
  (9 shorter events, 0.1 us)
Async XLA Ops:
  0.6 14.4 %collective-permute-start.3 = (bf16[8,56,128]{2,1,0:T(8,128)(2,1)}, bf16[8,56,128]{2,1,0:T(8,128)(2,1)S(1)}, u32[]{:S(2)}, u32[]{:S(2)}) collective-permute-start(bf16[8,56,128]{2,1,0:T(8,128)(2,1)} %bitcast.12), channel_id=1, source_target_pairs={{0,4},{1,5},{2,6},{3,7},{4,0},{5,1},{6,2},{7,3},{8,12},{9,13},{10,... | collective-permute-start | bytes 344072 | tf_op jit(solution)/shard_map/ppermute | solution.py:284
  7.9 7.1 %copy-start = (bf16[8,1,56,128]{3,2,1,0:T(8,128)(2,1)S(1)}, bf16[8,1,56,128]{3,2,1,0:T(8,128)(2,1)}, u32[]{:S(2)}) copy-start(bf16[8,1,56,128]{3,2,1,0:T(8,128)(2,1)} %param.4) | copy-start | bytes 344068
  9.7 10.9 %copy-start.1 = (bf16[10,56,128]{2,1,0:T(8,128)(2,1)S(1)}, bf16[10,56,128]{2,1,0:T(8,128)(2,1)}, u32[]{:S(2)}) copy-start(bf16[10,56,128]{2,1,0:T(8,128)(2,1)} %mask.1.m0) | copy-start | bytes 430084
  9.7 8.4 %collective-permute-start.2 = (bf16[10,56,128]{2,1,0:T(8,128)(2,1)}, bf16[10,56,128]{2,1,0:T(8,128)(2,1)S(1)}, u32[]{:S(2)}, u32[]{:S(2)}) collective-permute-start(bf16[10,56,128]{2,1,0:T(8,128)(2,1)} %mask.1.m0), channel_id=1, source_target_pairs={{0,2},{1,3},{2,0},{3,1},{4,6},{5,7},{6,4},{7,5},{8,10},{9,11},{10,... | collective-permute-start | bytes 430088 | tf_op jit(solution)/shard_map/ppermute | solution.py:286
  13.0 7.2 %collective-permute-start.1 = (bf16[10,56,128]{2,1,0:T(8,128)(2,1)}, bf16[10,56,128]{2,1,0:T(8,128)(2,1)S(1)}, u32[]{:S(2)}, u32[]{:S(2)}) collective-permute-start(bf16[10,56,128]{2,1,0:T(8,128)(2,1)} %mask.1.m0), channel_id=1, source_target_pairs={{0,3},{1,0},{2,1},{3,2},{4,7},{5,4},{6,5},{7,6},{8,11},{9,8},{10,9... | collective-permute-start | bytes 430088 | tf_op jit(solution)/shard_map/ppermute | solution.py:286
  14.0 6.5 %collective-permute-start = (bf16[10,56,128]{2,1,0:T(8,128)(2,1)}, bf16[10,56,128]{2,1,0:T(8,128)(2,1)S(1)}, u32[]{:S(2)}, u32[]{:S(2)}) collective-permute-start(bf16[10,56,128]{2,1,0:T(8,128)(2,1)} %mask.1.m0), channel_id=1, source_target_pairs={{0,1},{1,2},{2,3},{3,0},{4,5},{5,6},{6,7},{7,4},{8,9},{9,10},{10,1... | collective-permute-start | bytes 430088 | tf_op jit(solution)/shard_map/ppermute | solution.py:286
  15.0 9.5 %collective-permute-start.5 = (bf16[16,56,128]{2,1,0:T(8,128)(2,1)S(1)}, bf16[16,56,128]{2,1,0:T(8,128)(2,1)S(1)}, u32[]{:S(2)}, u32[]{:S(2)}) collective-permute-start(bf16[16,56,128]{2,1,0:T(8,128)(2,1)S(1)} %pad_maximum_fusion), channel_id=1, source_target_pairs={{8,16},{16,8},{24,32},{32,24},{40,48},{48,40},{56,64},{64,56},{72,... | collective-permute-start | bytes 688136 | tf_op jit(solution)/shard_map/ppermute | solution.py:291
  17.0 7.5 %collective-permute-start.4 = (bf16[16,56,128]{2,1,0:T(8,128)(2,1)S(1)}, bf16[16,56,128]{2,1,0:T(8,128)(2,1)S(1)}, u32[]{:S(2)}, u32[]{:S(2)}) collective-permute-start(bf16[16,56,128]{2,1,0:T(8,128)(2,1)S(1)} %pad_maximum_fusion), channel_id=1, source_target_pairs={{0,8},{8,0},{16,24},{24,16},{32,40},{40,32},{48,56},{56,48},{64,72... | collective-permute-start | bytes 688136 | tf_op jit(solution)/shard_map/ppermute | solution.py:291
  21.6 14.8 %collective-permute-start.10 = (f32[896,128]{1,0:T(8,128)S(1)}, f32[896,128]{1,0:T(8,128)S(1)}, u32[]{:S(2)}, u32[]{:S(2)}) collective-permute-start(f32[896,128]{1,0:T(8,128)S(1)} %get-tuple-element.18), channel_id=1, source_target_pairs={{0,8},{8,0},{16,24},{24,16},{32,40},{40,32},{48,56},{56,48},{64,72... | collective-permute-start | bytes 1376264 | tf_op jit(solution)/shard_map/ppermute | solution.py:296
  21.7 14.7 %collective-permute-start.11 = (f32[896,128]{1,0:T(8,128)S(1)}, f32[896,128]{1,0:T(8,128)S(1)}, u32[]{:S(2)}, u32[]{:S(2)}) collective-permute-start(f32[896,128]{1,0:T(8,128)S(1)} %get-tuple-element.19), channel_id=1, source_target_pairs={{8,16},{16,8},{24,32},{32,24},{40,48},{48,40},{56,64},{64,56},{72,... | collective-permute-start | bytes 1376264 | tf_op jit(solution)/shard_map/ppermute | solution.py:296
  25.7 1.3 %collective-permute-start.6 = (f32[96,128]{1,0:T(8,128)S(1)}, f32[96,128]{1,0:T(8,128)S(1)}, u32[]{:S(2)}, u32[]{:S(2)}) collective-permute-start(f32[96,128]{1,0:T(8,128)S(1)} %get-tuple-element.16), channel_id=1, source_target_pairs={{0,8},{8,0},{16,24},{24,16},{32,40},{40,32},{48,56},{56,48},{64,72... | collective-permute-start | bytes 147464 | tf_op jit(solution)/shard_map/ppermute | solution.py:294
  27.0 7.2 %collective-permute-start.9 = (f32[96,128]{1,0:T(8,128)S(1)}, f32[96,128]{1,0:T(8,128)S(1)}, u32[]{:S(2)}, u32[]{:S(2)}) collective-permute-start(f32[96,128]{1,0:T(8,128)S(1)} %add.30), channel_id=1, source_target_pairs={{0,32},{8,40},{16,48},{24,56},{32,0},{40,8},{48,16},{56,24},{64,96... | collective-permute-start | bytes 147464 | tf_op jit(solution)/shard_map/ppermute | solution.py:295
  28.8 7.6 %collective-permute-start.8 = (f32[96,128]{1,0:T(8,128)S(1)}, f32[96,128]{1,0:T(8,128)S(1)}, u32[]{:S(2)}, u32[]{:S(2)}) collective-permute-start(f32[96,128]{1,0:T(8,128)S(1)} %add.30), channel_id=1, source_target_pairs={{0,48},{8,56},{16,0},{24,8},{32,16},{40,24},{48,32},{56,40},{64,11... | collective-permute-start | bytes 147464 | tf_op jit(solution)/shard_map/ppermute | solution.py:295
  28.8 7.6 %collective-permute-start.7 = (f32[96,128]{1,0:T(8,128)S(1)}, f32[96,128]{1,0:T(8,128)S(1)}, u32[]{:S(2)}, u32[]{:S(2)}) collective-permute-start(f32[96,128]{1,0:T(8,128)S(1)} %add.30), channel_id=1, source_target_pairs={{0,16},{8,24},{16,32},{24,40},{32,48},{40,56},{48,0},{56,8},{64,80... | collective-permute-start | bytes 147464 | tf_op jit(solution)/shard_map/ppermute | solution.py:295
  36.5 6.6 %collective-permute-start.15 = (f32[96,128]{1,0:T(8,128)S(1)}, f32[96,128]{1,0:T(8,128)S(1)}, u32[]{:S(2)}, u32[]{:S(2)}) collective-permute-start(f32[96,128]{1,0:T(8,128)S(1)} %add_add_fusion.2), channel_id=1, source_target_pairs={{0,192},{8,200},{16,208},{24,216},{32,224},{40,232},{48,240},{56,2... | collective-permute-start | bytes 147464 | tf_op jit(solution)/shard_map/ppermute | solution.py:298
  37.0 7.4 %collective-permute-start.14 = (f32[96,128]{1,0:T(8,128)S(1)}, f32[96,128]{1,0:T(8,128)S(1)}, u32[]{:S(2)}, u32[]{:S(2)}) collective-permute-start(f32[96,128]{1,0:T(8,128)S(1)} %add_add_fusion.2), channel_id=1, source_target_pairs={{0,128},{8,136},{16,144},{24,152},{32,160},{40,168},{48,176},{56,1... | collective-permute-start | bytes 147464 | tf_op jit(solution)/shard_map/ppermute | solution.py:298
  39.0 7.7 %collective-permute-start.13 = (f32[96,128]{1,0:T(8,128)S(1)}, f32[96,128]{1,0:T(8,128)S(1)}, u32[]{:S(2)}, u32[]{:S(2)}) collective-permute-start(f32[96,128]{1,0:T(8,128)S(1)} %add_add_fusion.2), channel_id=1, source_target_pairs={{0,64},{8,72},{16,80},{24,88},{32,96},{40,104},{48,112},{56,120},{... | collective-permute-start | bytes 147464 | tf_op jit(solution)/shard_map/ppermute | solution.py:298
  41.0 15.4 %collective-permute-start.12 = (f32[448,128]{1,0:T(8,128)S(1)}, f32[448,128]{1,0:T(8,128)S(1)}, u32[]{:S(2)}, u32[]{:S(2)}) collective-permute-start(f32[448,128]{1,0:T(8,128)S(1)} %slice.19), channel_id=1, source_target_pairs={{0,4},{1,5},{2,6},{3,7},{4,0},{5,1},{6,2},{7,3},{8,12},{9,13},{10,... | collective-permute-start | bytes 688136 | tf_op jit(solution)/shard_map/ppermute | solution.py:307
  46.7 5.3 %collective-permute-start.18 = (f32[24,128]{1,0:T(8,128)S(1)}, f32[24,128]{1,0:T(8,128)S(1)}, u32[]{:S(2)}, u32[]{:S(2)}) collective-permute-start(f32[24,128]{1,0:T(8,128)S(1)} %get-tuple-element.25), channel_id=1, source_target_pairs={{0,2},{1,3},{2,0},{3,1},{4,6},{5,7},{6,4},{7,5},{8,10},{9,11},{10,... | collective-permute-start | bytes 36872 | tf_op jit(solution)/shard_map/ppermute | solution.py:300
  46.8 5.2 %collective-permute-start.17 = (f32[24,128]{1,0:T(8,128)S(1)}, f32[24,128]{1,0:T(8,128)S(1)}, u32[]{:S(2)}, u32[]{:S(2)}) collective-permute-start(f32[24,128]{1,0:T(8,128)S(1)} %get-tuple-element.26), channel_id=1, source_target_pairs={{0,1},{1,2},{2,3},{3,0},{4,5},{5,6},{6,7},{7,4},{8,9},{9,10},{10,1... | collective-permute-start | bytes 36872 | tf_op jit(solution)/shard_map/ppermute | solution.py:300
  47.1 4.9 %collective-permute-start.16 = (f32[24,128]{1,0:T(8,128)S(1)}, f32[24,128]{1,0:T(8,128)S(1)}, u32[]{:S(2)}, u32[]{:S(2)}) collective-permute-start(f32[24,128]{1,0:T(8,128)S(1)} %get-tuple-element.27), channel_id=1, source_target_pairs={{0,3},{1,0},{2,1},{3,2},{4,7},{5,4},{6,5},{7,6},{8,11},{9,8},{10,9... | collective-permute-start | bytes 36872 | tf_op jit(solution)/shard_map/ppermute | solution.py:300
  52.0 1.3 %collective-permute-start.19 = (f32[96,128]{1,0:T(8,128)S(1)}, f32[96,128]{1,0:T(8,128)S(1)}, u32[]{:S(2)}, u32[]{:S(2)}) collective-permute-start(f32[96,128]{1,0:T(8,128)S(1)} %pad_maximum_fusion.1.refs_0_), channel_id=1, source_target_pairs={{0,8},{8,0},{16,24},{24,16},{32,40},{40,32},{48,56},{56,48},{64,72... | collective-permute-start | bytes 147464 | tf_op jit(solution)/shard_map/ppermute | solution.py:302

commit v3 on v2

--- a/solution.py
+++ b/solution.py
@@ -116,6 +116,20 @@
             pieces += column_shifts(scratch, row, lane)
         columns.append(jnp.concatenate(pieces, axis=0).astype(BF))
     return jnp.concatenate(columns, axis=1)
+
+
+def packed(part, lane):
+    tiles = []
+    for j in range(4):
+        one, two, three = (part[24 * j + 8 * kx : 24 * j + 8 * kx + 8] for kx in range(3))
+        two = pltpu.roll(two, 72, 1)
+        tiles += [jnp.where(lane < 72, one, two), jnp.where(lane < 16, two, pltpu.roll(three, 16, 1))]
+    return jnp.concatenate(tiles, axis=0)
+
+
+def unpacked(left, right, lane):
+    two = jnp.where(lane < 56, pltpu.roll(left, 56, 1), pltpu.roll(right, 56, 1))
+    return jnp.concatenate([left, two, pltpu.roll(right, 112, 1)], axis=0)
 
 
 def weight_body(m0, m1, m2, m3, *refs):
@@ -155,13 +169,13 @@
         total = total + lax.dot_general(
             lhs, rhs, (((1,), (1,)), ((), ())), preferred_element_type=F32
         )
-    own, other = total[:, :COLS], total[:, COLS:]
+    own, other = packed(total[:, :COLS], lane), packed(total[:, COLS:], lane)
     keep_ref[...] = jnp.where(first_core, own, other)
     send_ref[...] = jnp.where(first_core, other, own)
 
 
 def weight_call(masked, acts):
-    shape = jax.ShapeDtypeStruct((96, COLS), F32)
+    shape = jax.ShapeDtypeStruct((64, COLS), F32)
     return pl.pallas_call(
         weight_body,
         out_shape=(shape, shape),
@@ -252,7 +266,8 @@
     for ref, part in ((mine_ref, half ^ core), (theirs_ref, half ^ core ^ 1)):
         for j, away in enumerate((0, 1, 3, 2)):
             block = 4 * part + lax.rem(y + away, 4)
-            sources.append((block, ref[24 * j : 24 * j + 24]))
+            left, right = ref[16 * j : 16 * j + 8], ref[16 * j + 8 : 16 * j + 16]
+            sources.append((block, unpacked(left, right, lane[:8])))
     for q in range(9):
         total = jnp.zeros((24, COLS), F32)
         for block, value in sources:
@@ -296,7 +311,7 @@
     layer = mid + lax.ppermute(to_inner, "space", CORE) + lax.ppermute(to_outer, "space", OUTER)
     terms, layer = lax.optimization_barrier((terms, layer))
     terms = sum([lax.ppermute(terms, "space", pairs) for pairs in Z_OTHERS], terms)
-    blocks = [terms[24 * j : 24 * j + 24] for j in range(4)]
+    blocks = [terms[16 * j : 16 * j + 16] for j in range(4)]
     got = [lax.ppermute(block, "filt", pairs) for block, pairs in zip(blocks[1:], Y_BACK)]
     mine_blocks = jnp.concatenate([blocks[0]] + got, axis=0)
     their_blocks = lax.ppermute(mine_blocks, "space", CORE)

time: 57.1 us -> 58.9 us (1.032)
  the two profiles are of different devices: /device:TPU:6 before, /device:TPU:105 now
where the time goes in v3:
time: 58.9 us; the launch traced here: 58.7 us
  starting transfers between devices  44.7 us (76%)
  waiting for transfers between devices  7.36 us (12%)
  Pallas kernels  5.03 us (9%)
  other arithmetic  0.79 us (1%)
  between operations  0.77 us (1%)
    ppermute x1, starting transfers between devices, on_device(): their_blocks = lax.ppermute(mine_blocks, 'space', CORE)  12.8 us
    ppermute x6, starting transfers between devices, on_device(): lax.ppermute(terms, 'space', pairs)  5.69 us
    ppermute x1, starting transfers between devices, on_device(): lax.ppermute(both, 'space', OUTER)  4.8 us
    ppermute x1, starting transfers between devices, on_device(): other = lax.ppermute(acts, 'filt', HALF)  4.3 us
    ppermute x6, waiting for transfers between devices, on_device(): lax.ppermute(terms, 'space', pairs)  3.67 us
    ppermute x3, starting transfers between devices, on_device(): lax.ppermute(block, 'filt', pairs)  3.57 us
    ppermute x3, starting transfers between devices, on_device(): masked = [mine] + [lax.ppermute(mine, 'filt', pairs) for pairs in Y_OTHERS]  3.57 us
    ppermute x1, starting transfers between devices, on_device(): lax.ppermute(to_outer, 'space', OUTER)  3.02 us
  transfers between devices with their start and end apart: 20, of which 7 were waited for; matrix products, arithmetic and copies ran while one was open for 0% of the time, Pallas kernels for 9%

profile of v3, /device:TPU:105, one launch (start us, length us, event | category | flops | bytes accessed | tf_op | source)
XLA Modules:
  0.0 58.7 jit_solution(12805590136485356661)
XLA Ops:
  0.6 4.3 %collective-permute-start.3 = (bf16[8,56,128]{2,1,0:T(8,128)(2,1)}, bf16[8,56,128]{2,1,0:T(8,128)(2,1)S(1)}, u32[]{:S(2)}, u32[]{:S(2)}) collective-permute-start(bf16[8,56,128]{2,1,0:T(8,128)(2,1)} %bitcast.12), channel_id=1, source_target_pairs={{0,4},{1,5},{2,6},{3,7},{4,0},{5,1},{6,2},{7,3},{8,12},{9,13},{10,... | collective-permute-start | bytes 344072 | tf_op jit(solution)/shard_map/ppermute | solution.py:299
  4.9 1.8 %mask.1.m0 = bf16[10,56,128]{2,1,0:T(8,128)(2,1)} custom-call(bf16[8,56,128]{2,1,0:T(8,128)(2,1)} %bitcast.17, bf16[8,56,128]{2,1,0:T(8,128)(2,1)} %bitcast.18, bf16[27,8,64]{2,1,0:T(8,128)(2,1)} %bitcast.19), custom_call_target="tpu_custom_call" | custom-call | flops 20000000000 | bytes 500000 | tf_op jit(solution)/shard_map/mask/pallas_call | solution.py:73
  6.7 0.0 copy-start.1
  6.7 2.1 %collective-permute-start.2 = (bf16[10,56,128]{2,1,0:T(8,128)(2,1)}, bf16[10,56,128]{2,1,0:T(8,128)(2,1)S(1)}, u32[]{:S(2)}, u32[]{:S(2)}) collective-permute-start(bf16[10,56,128]{2,1,0:T(8,128)(2,1)} %mask.1.m0), channel_id=1, source_target_pairs={{0,2},{1,3},{2,0},{3,1},{4,6},{5,7},{6,4},{7,5},{8,10},{9,11},{10,... | collective-permute-start | bytes 430088 | tf_op jit(solution)/shard_map/ppermute | solution.py:301
  8.8 1.1 %collective-permute-start.1 = (bf16[10,56,128]{2,1,0:T(8,128)(2,1)}, bf16[10,56,128]{2,1,0:T(8,128)(2,1)S(1)}, u32[]{:S(2)}, u32[]{:S(2)}) collective-permute-start(bf16[10,56,128]{2,1,0:T(8,128)(2,1)} %mask.1.m0), channel_id=1, source_target_pairs={{0,3},{1,0},{2,1},{3,2},{4,7},{5,4},{6,5},{7,6},{8,11},{9,8},{10,9... | collective-permute-start | bytes 430088 | tf_op jit(solution)/shard_map/ppermute | solution.py:301
  9.9 0.4 collective-permute-start
  10.3 0.0 collective-permute-done.3.refs_1_
  10.3 0.0 copy-done
  10.3 4.8 %collective-permute-start.5 = (bf16[16,56,128]{2,1,0:T(8,128)(2,1)S(1)}, bf16[16,56,128]{2,1,0:T(8,128)(2,1)S(1)}, u32[]{:S(2)}, u32[]{:S(2)}) collective-permute-start(bf16[16,56,128]{2,1,0:T(8,128)(2,1)S(1)} %pad_maximum_fusion), channel_id=1, source_target_pairs={{8,16},{16,8},{24,32},{32,24},{40,48},{48,40},{56,64},{64,56},{72,... | collective-permute-start | bytes 688136 | tf_op jit(solution)/shard_map/ppermute | solution.py:306
  15.1 1.0 %collective-permute-start.4 = (bf16[16,56,128]{2,1,0:T(8,128)(2,1)S(1)}, bf16[16,56,128]{2,1,0:T(8,128)(2,1)S(1)}, u32[]{:S(2)}, u32[]{:S(2)}) collective-permute-start(bf16[16,56,128]{2,1,0:T(8,128)(2,1)S(1)} %pad_maximum_fusion), channel_id=1, source_target_pairs={{0,8},{8,0},{16,24},{24,16},{32,40},{40,32},{48,56},{56,48},{64,72... | collective-permute-start | bytes 688136 | tf_op jit(solution)/shard_map/ppermute | solution.py:306
  16.2 0.0 collective-permute-done.2.m3
  16.2 0.9 %collective-permute-done.1.m2 = bf16[10,56,128]{2,1,0:T(8,128)(2,1)S(1)} collective-permute-done((bf16[10,56,128]{2,1,0:T(8,128)(2,1)}, bf16[10,56,128]{2,1,0:T(8,128)(2,1)S(1)}, u32[]{:S(2)}, u32[]{:S(2)}) %collective-permute-start.1) | collective-permute-done | bytes 143392 | tf_op jit(solution)/shard_map/ppermute | solution.py:301
  17.1 0.0 collective-permute-done.m1
  17.1 1.0 %data_grad.1 = (f32[896,128]{1,0:T(8,128)S(1)}, f32[896,128]{1,0:T(8,128)S(1)}, f32[896,128]{1,0:T(8,128)S(1)}) custom-call(bf16[10,56,128]{2,1,0:T(8,128)(2,1)S(1)} %copy-done.1, bf16[10,56,128]{2,1,0:T(8,128)(2,1)S(1)} %collective-permute-done.m1, bf16[10,56,128]{2,1,0:T(8,128)(2,1)S(1)} %collective-permute-done.1.m2, ...), custom_call_target="tpu_custom_call" | custom-call | flops 20000000000 | bytes 2000000 | tf_op jit(solution)/shard_map/data_grad/pallas_call | solution.py:248
  18.1 0.9 %collective-permute-start.10 = (f32[896,128]{1,0:T(8,128)S(1)}, f32[896,128]{1,0:T(8,128)S(1)}, u32[]{:S(2)}, u32[]{:S(2)}) collective-permute-start(f32[896,128]{1,0:T(8,128)S(1)} %get-tuple-element.18), channel_id=1, source_target_pairs={{0,8},{8,0},{16,24},{24,16},{32,40},{40,32},{48,56},{56,48},{64,72... | collective-permute-start | bytes 1376264 | tf_op jit(solution)/shard_map/ppermute | solution.py:311
  19.0 3.0 %collective-permute-start.11 = (f32[896,128]{1,0:T(8,128)S(1)}, f32[896,128]{1,0:T(8,128)S(1)}, u32[]{:S(2)}, u32[]{:S(2)}) collective-permute-start(f32[896,128]{1,0:T(8,128)S(1)} %get-tuple-element.19), channel_id=1, source_target_pairs={{8,16},{16,8},{24,32},{32,24},{40,48},{48,40},{56,64},{64,56},{72,... | collective-permute-start | bytes 1376264 | tf_op jit(solution)/shard_map/ppermute | solution.py:311
  22.0 0.0 collective-permute-done.5.refs_3_
  22.0 0.0 collective-permute-done.4.refs_2_
  22.0 1.2 %weight_grad.1 = (f32[64,128]{1,0:T(8,128)S(1)}, f32[64,128]{1,0:T(8,128)S(1)}) custom-call(bf16[10,56,128]{2,1,0:T(8,128)(2,1)S(1)} %copy-done.1, bf16[10,56,128]{2,1,0:T(8,128)(2,1)S(1)} %collective-permute-done.m1, bf16[10,56,128]{2,1,0:T(8,128)(2,1)S(1)} %collective-permute-done.1.m2, bf16[10,56,128]{2,1,0:T(8,128)(2,1)S(1)} %collective-permute-done.2.m3, ...), custom_call_target="tpu_custom_call" | custom-call | flops 20000000000 | bytes 1500000 | tf_op jit(solution)/shard_map/weight_grad/pallas_call | solution.py:179
  23.3 2.3 %collective-permute-start.6 = (f32[64,128]{1,0:T(8,128)S(1)}, f32[64,128]{1,0:T(8,128)S(1)}, u32[]{:S(2)}, u32[]{:S(2)}) collective-permute-start(f32[64,128]{1,0:T(8,128)S(1)} %get-tuple-element.16), channel_id=1, source_target_pairs={{0,8},{8,0},{16,24},{24,16},{32,40},{40,32},{48,56},{56,48},{64,72... | collective-permute-start | bytes 98312 | tf_op jit(solution)/shard_map/ppermute | solution.py:309
  25.6 0.9 %collective-permute-done.6 = f32[64,128]{1,0:T(8,128)S(1)} collective-permute-done((f32[64,128]{1,0:T(8,128)S(1)}, f32[64,128]{1,0:T(8,128)S(1)}, u32[]{:S(2)}, u32[]{:S(2)}) %collective-permute-start.6) | collective-permute-done | bytes 32800 | tf_op jit(solution)/shard_map/ppermute | solution.py:309
  26.4 0.6 %collective-permute-start.9 = (f32[64,128]{1,0:T(8,128)S(1)}, f32[64,128]{1,0:T(8,128)S(1)}, u32[]{:S(2)}, u32[]{:S(2)}) collective-permute-start(f32[64,128]{1,0:T(8,128)S(1)} %add.30), channel_id=1, source_target_pairs={{0,32},{8,40},{16,48},{24,56},{32,0},{40,8},{48,16},{56,24},{64,96... | collective-permute-start | bytes 98312 | tf_op jit(solution)/shard_map/ppermute | solution.py:310
  27.0 1.2 %collective-permute-start.8 = (f32[64,128]{1,0:T(8,128)S(1)}, f32[64,128]{1,0:T(8,128)S(1)}, u32[]{:S(2)}, u32[]{:S(2)}) collective-permute-start(f32[64,128]{1,0:T(8,128)S(1)} %add.30), channel_id=1, source_target_pairs={{0,48},{8,56},{16,0},{24,8},{32,16},{40,24},{48,32},{56,40},{64,11... | collective-permute-start | bytes 98312 | tf_op jit(solution)/shard_map/ppermute | solution.py:310
  28.2 0.3 collective-permute-start.7
  28.5 2.2 %collective-permute-done.9 = f32[64,128]{1,0:T(8,128)S(1)} collective-permute-done((f32[64,128]{1,0:T(8,128)S(1)}, f32[64,128]{1,0:T(8,128)S(1)}, u32[]{:S(2)}, u32[]{:S(2)}) %collective-permute-start.9) | collective-permute-done | bytes 32800 | tf_op jit(solution)/shard_map/ppermute | solution.py:310
  30.7 0.0 collective-permute-done.8
  30.7 1.5 %collective-permute-done.7 = f32[64,128]{1,0:T(8,128)S(1)} collective-permute-done((f32[64,128]{1,0:T(8,128)S(1)}, f32[64,128]{1,0:T(8,128)S(1)}, u32[]{:S(2)}, u32[]{:S(2)}) %collective-permute-start.7) | collective-permute-done | bytes 32800 | tf_op jit(solution)/shard_map/ppermute | solution.py:310
  32.2 0.0 collective-permute-done.10
  32.2 0.0 collective-permute-done.11
  32.2 0.1 add_add_fusion
  32.3 1.7 %collective-permute-start.15 = (f32[64,128]{1,0:T(8,128)S(1)}, f32[64,128]{1,0:T(8,128)S(1)}, u32[]{:S(2)}, u32[]{:S(2)}) collective-permute-start(f32[64,128]{1,0:T(8,128)S(1)} %add_add_fusion.2), channel_id=1, source_target_pairs={{0,192},{8,200},{16,208},{24,216},{32,224},{40,232},{48,240},{56,2... | collective-permute-start | bytes 98312 | tf_op jit(solution)/shard_map/ppermute | solution.py:313
  34.0 0.3 collective-permute-start.14
  34.3 1.6 %collective-permute-start.13 = (f32[64,128]{1,0:T(8,128)S(1)}, f32[64,128]{1,0:T(8,128)S(1)}, u32[]{:S(2)}, u32[]{:S(2)}) collective-permute-start(f32[64,128]{1,0:T(8,128)S(1)} %add_add_fusion.2), channel_id=1, source_target_pairs={{0,64},{8,72},{16,80},{24,88},{32,96},{40,104},{48,112},{56,120},{... | collective-permute-start | bytes 98312 | tf_op jit(solution)/shard_map/ppermute | solution.py:313
  35.9 2.8 %collective-permute-start.12 = (f32[448,128]{1,0:T(8,128)S(1)}, f32[448,128]{1,0:T(8,128)S(1)}, u32[]{:S(2)}, u32[]{:S(2)}) collective-permute-start(f32[448,128]{1,0:T(8,128)S(1)} %slice.19), channel_id=1, source_target_pairs={{0,4},{1,5},{2,6},{3,7},{4,0},{5,1},{6,2},{7,3},{8,12},{9,13},{10,... | collective-permute-start | bytes 688136 | tf_op jit(solution)/shard_map/ppermute | solution.py:322
  38.7 0.0 collective-permute-done.15
  38.7 0.0 collective-permute-done.14
  38.7 0.0 collective-permute-done.13
  38.7 2.1 %collective-permute-start.18 = (f32[16,128]{1,0:T(8,128)S(1)}, f32[16,128]{1,0:T(8,128)S(1)}, u32[]{:S(2)}, u32[]{:S(2)}) collective-permute-start(f32[16,128]{1,0:T(8,128)S(1)} %get-tuple-element.25), channel_id=1, source_target_pairs={{0,2},{1,3},{2,0},{3,1},{4,6},{5,7},{6,4},{7,5},{8,10},{9,11},{10,... | collective-permute-start | bytes 24584 | tf_op jit(solution)/shard_map/ppermute | solution.py:315
  40.8 0.0 collective-permute-start.17
  40.8 1.5 %collective-permute-start.16 = (f32[16,128]{1,0:T(8,128)S(1)}, f32[16,128]{1,0:T(8,128)S(1)}, u32[]{:S(2)}, u32[]{:S(2)}) collective-permute-start(f32[16,128]{1,0:T(8,128)S(1)} %get-tuple-element.27), channel_id=1, source_target_pairs={{0,3},{1,0},{2,1},{3,2},{4,7},{5,4},{6,5},{7,6},{8,11},{9,8},{10,9... | collective-permute-start | bytes 24584 | tf_op jit(solution)/shard_map/ppermute | solution.py:315
  42.3 0.5 collective-permute-done.18
  42.8 0.5 collective-permute-done.17
  43.3 0.0 collective-permute-done.16
  43.3 12.8 %collective-permute-start.19 = (f32[64,128]{1,0:T(8,128)S(1)}, f32[64,128]{1,0:T(8,128)S(1)}, u32[]{:S(2)}, u32[]{:S(2)}) collective-permute-start(f32[64,128]{1,0:T(8,128)S(1)} %pad_maximum_fusion.1.refs_0_), channel_id=1, source_target_pairs={{0,8},{8,0},{16,24},{24,16},{32,40},{40,32},{48,56},{56,48},{64,72... | collective-permute-start | bytes 98312 | tf_op jit(solution)/shard_map/ppermute | solution.py:317
  56.2 0.9 %collective-permute-done.19.refs_1_ = f32[64,128]{1,0:T(8,128)S(1)} collective-permute-done((f32[64,128]{1,0:T(8,128)S(1)}, f32[64,128]{1,0:T(8,128)S(1)}, u32[]{:S(2)}, u32[]{:S(2)}) %collective-permute-start.19) | collective-permute-done | bytes 32800 | tf_op jit(solution)/shard_map/ppermute | solution.py:317
  57.0 1.0 %place_blocks.1 = f32[216,64]{1,0:T(8,128)} custom-call(f32[64,128]{1,0:T(8,128)S(1)} %pad_maximum_fusion.1.refs_0_, f32[64,128]{1,0:T(8,128)S(1)} %collective-permute-done.19.refs_1_), custom_call_target="tpu_custom_call" | custom-call | flops 100000 | bytes 200000 | tf_op jit(solution)/shard_map/place_blocks/pallas_call | solution.py:281
  58.0 0.0 collective-permute-done.12
  58.0 0.7 %add_convert_fusion = bf16[448,128]{1,0:T(8,128)(2,1)} fusion(f32[448,128]{1,0:T(8,128)S(1)} %collective-permute-done.12, f32[896,128]{1,0:T(8,128)S(1)} %add_add_fusion), kind=kLoop, calls=%fused_computation.2 | loop fusion | flops 114688 | bytes 573440 | tf_op jit(solution)/shard_map/convert_element_type | solution.py:323
  (9 shorter events, 0.1 us)
Async XLA Ops:
  0.6 9.7 %collective-permute-start.3 = (bf16[8,56,128]{2,1,0:T(8,128)(2,1)}, bf16[8,56,128]{2,1,0:T(8,128)(2,1)S(1)}, u32[]{:S(2)}, u32[]{:S(2)}) collective-permute-start(bf16[8,56,128]{2,1,0:T(8,128)(2,1)} %bitcast.12), channel_id=1, source_target_pairs={{0,4},{1,5},{2,6},{3,7},{4,0},{5,1},{6,2},{7,3},{8,12},{9,13},{10,... | collective-permute-start | bytes 344072 | tf_op jit(solution)/shard_map/ppermute | solution.py:299
  4.9 5.4 %copy-start = (bf16[8,1,56,128]{3,2,1,0:T(8,128)(2,1)S(1)}, bf16[8,1,56,128]{3,2,1,0:T(8,128)(2,1)}, u32[]{:S(2)}) copy-start(bf16[8,1,56,128]{3,2,1,0:T(8,128)(2,1)} %param.4) | copy-start | bytes 344068
  6.7 10.4 %copy-start.1 = (bf16[10,56,128]{2,1,0:T(8,128)(2,1)S(1)}, bf16[10,56,128]{2,1,0:T(8,128)(2,1)}, u32[]{:S(2)}) copy-start(bf16[10,56,128]{2,1,0:T(8,128)(2,1)} %mask.1.m0) | copy-start | bytes 430084
  6.7 9.4 %collective-permute-start.2 = (bf16[10,56,128]{2,1,0:T(8,128)(2,1)}, bf16[10,56,128]{2,1,0:T(8,128)(2,1)S(1)}, u32[]{:S(2)}, u32[]{:S(2)}) collective-permute-start(bf16[10,56,128]{2,1,0:T(8,128)(2,1)} %mask.1.m0), channel_id=1, source_target_pairs={{0,2},{1,3},{2,0},{3,1},{4,6},{5,7},{6,4},{7,5},{8,10},{9,11},{10,... | collective-permute-start | bytes 430088 | tf_op jit(solution)/shard_map/ppermute | solution.py:301
  8.8 8.2 %collective-permute-start.1 = (bf16[10,56,128]{2,1,0:T(8,128)(2,1)}, bf16[10,56,128]{2,1,0:T(8,128)(2,1)S(1)}, u32[]{:S(2)}, u32[]{:S(2)}) collective-permute-start(bf16[10,56,128]{2,1,0:T(8,128)(2,1)} %mask.1.m0), channel_id=1, source_target_pairs={{0,3},{1,0},{2,1},{3,2},{4,7},{5,4},{6,5},{7,6},{8,11},{9,8},{10,9... | collective-permute-start | bytes 430088 | tf_op jit(solution)/shard_map/ppermute | solution.py:301
  9.9 7.2 %collective-permute-start = (bf16[10,56,128]{2,1,0:T(8,128)(2,1)}, bf16[10,56,128]{2,1,0:T(8,128)(2,1)S(1)}, u32[]{:S(2)}, u32[]{:S(2)}) collective-permute-start(bf16[10,56,128]{2,1,0:T(8,128)(2,1)} %mask.1.m0), channel_id=1, source_target_pairs={{0,1},{1,2},{2,3},{3,0},{4,5},{5,6},{6,7},{7,4},{8,9},{9,10},{10,1... | collective-permute-start | bytes 430088 | tf_op jit(solution)/shard_map/ppermute | solution.py:301
  10.3 11.7 %collective-permute-start.5 = (bf16[16,56,128]{2,1,0:T(8,128)(2,1)S(1)}, bf16[16,56,128]{2,1,0:T(8,128)(2,1)S(1)}, u32[]{:S(2)}, u32[]{:S(2)}) collective-permute-start(bf16[16,56,128]{2,1,0:T(8,128)(2,1)S(1)} %pad_maximum_fusion), channel_id=1, source_target_pairs={{8,16},{16,8},{24,32},{32,24},{40,48},{48,40},{56,64},{64,56},{72,... | collective-permute-start | bytes 688136 | tf_op jit(solution)/shard_map/ppermute | solution.py:306
  15.1 6.9 %collective-permute-start.4 = (bf16[16,56,128]{2,1,0:T(8,128)(2,1)S(1)}, bf16[16,56,128]{2,1,0:T(8,128)(2,1)S(1)}, u32[]{:S(2)}, u32[]{:S(2)}) collective-permute-start(bf16[16,56,128]{2,1,0:T(8,128)(2,1)S(1)} %pad_maximum_fusion), channel_id=1, source_target_pairs={{0,8},{8,0},{16,24},{24,16},{32,40},{40,32},{48,56},{56,48},{64,72... | collective-permute-start | bytes 688136 | tf_op jit(solution)/shard_map/ppermute | solution.py:306
  18.1 14.1 %collective-permute-start.10 = (f32[896,128]{1,0:T(8,128)S(1)}, f32[896,128]{1,0:T(8,128)S(1)}, u32[]{:S(2)}, u32[]{:S(2)}) collective-permute-start(f32[896,128]{1,0:T(8,128)S(1)} %get-tuple-element.18), channel_id=1, source_target_pairs={{0,8},{8,0},{16,24},{24,16},{32,40},{40,32},{48,56},{56,48},{64,72... | collective-permute-start | bytes 1376264 | tf_op jit(solution)/shard_map/ppermute | solution.py:311
  19.0 13.2 %collective-permute-start.11 = (f32[896,128]{1,0:T(8,128)S(1)}, f32[896,128]{1,0:T(8,128)S(1)}, u32[]{:S(2)}, u32[]{:S(2)}) collective-permute-start(f32[896,128]{1,0:T(8,128)S(1)} %get-tuple-element.19), channel_id=1, source_target_pairs={{8,16},{16,8},{24,32},{32,24},{40,48},{48,40},{56,64},{64,56},{72,... | collective-permute-start | bytes 1376264 | tf_op jit(solution)/shard_map/ppermute | solution.py:311
  23.3 3.2 %collective-permute-start.6 = (f32[64,128]{1,0:T(8,128)S(1)}, f32[64,128]{1,0:T(8,128)S(1)}, u32[]{:S(2)}, u32[]{:S(2)}) collective-permute-start(f32[64,128]{1,0:T(8,128)S(1)} %get-tuple-element.16), channel_id=1, source_target_pairs={{0,8},{8,0},{16,24},{24,16},{32,40},{40,32},{48,56},{56,48},{64,72... | collective-permute-start | bytes 98312 | tf_op jit(solution)/shard_map/ppermute | solution.py:309
  26.4 4.3 %collective-permute-start.9 = (f32[64,128]{1,0:T(8,128)S(1)}, f32[64,128]{1,0:T(8,128)S(1)}, u32[]{:S(2)}, u32[]{:S(2)}) collective-permute-start(f32[64,128]{1,0:T(8,128)S(1)} %add.30), channel_id=1, source_target_pairs={{0,32},{8,40},{16,48},{24,56},{32,0},{40,8},{48,16},{56,24},{64,96... | collective-permute-start | bytes 98312 | tf_op jit(solution)/shard_map/ppermute | solution.py:310
  27.0 3.7 %collective-permute-start.8 = (f32[64,128]{1,0:T(8,128)S(1)}, f32[64,128]{1,0:T(8,128)S(1)}, u32[]{:S(2)}, u32[]{:S(2)}) collective-permute-start(f32[64,128]{1,0:T(8,128)S(1)} %add.30), channel_id=1, source_target_pairs={{0,48},{8,56},{16,0},{24,8},{32,16},{40,24},{48,32},{56,40},{64,11... | collective-permute-start | bytes 98312 | tf_op jit(solution)/shard_map/ppermute | solution.py:310
  28.2 4.0 %collective-permute-start.7 = (f32[64,128]{1,0:T(8,128)S(1)}, f32[64,128]{1,0:T(8,128)S(1)}, u32[]{:S(2)}, u32[]{:S(2)}) collective-permute-start(f32[64,128]{1,0:T(8,128)S(1)} %add.30), channel_id=1, source_target_pairs={{0,16},{8,24},{16,32},{24,40},{32,48},{40,56},{48,0},{56,8},{64,80... | collective-permute-start | bytes 98312 | tf_op jit(solution)/shard_map/ppermute | solution.py:310
  32.3 6.4 %collective-permute-start.15 = (f32[64,128]{1,0:T(8,128)S(1)}, f32[64,128]{1,0:T(8,128)S(1)}, u32[]{:S(2)}, u32[]{:S(2)}) collective-permute-start(f32[64,128]{1,0:T(8,128)S(1)} %add_add_fusion.2), channel_id=1, source_target_pairs={{0,192},{8,200},{16,208},{24,216},{32,224},{40,232},{48,240},{56,2... | collective-permute-start | bytes 98312 | tf_op jit(solution)/shard_map/ppermute | solution.py:313
  34.0 4.7 %collective-permute-start.14 = (f32[64,128]{1,0:T(8,128)S(1)}, f32[64,128]{1,0:T(8,128)S(1)}, u32[]{:S(2)}, u32[]{:S(2)}) collective-permute-start(f32[64,128]{1,0:T(8,128)S(1)} %add_add_fusion.2), channel_id=1, source_target_pairs={{0,128},{8,136},{16,144},{24,152},{32,160},{40,168},{48,176},{56,1... | collective-permute-start | bytes 98312 | tf_op jit(solution)/shard_map/ppermute | solution.py:313
  34.3 4.4 %collective-permute-start.13 = (f32[64,128]{1,0:T(8,128)S(1)}, f32[64,128]{1,0:T(8,128)S(1)}, u32[]{:S(2)}, u32[]{:S(2)}) collective-permute-start(f32[64,128]{1,0:T(8,128)S(1)} %add_add_fusion.2), channel_id=1, source_target_pairs={{0,64},{8,72},{16,80},{24,88},{32,96},{40,104},{48,112},{56,120},{... | collective-permute-start | bytes 98312 | tf_op jit(solution)/shard_map/ppermute | solution.py:313
  35.9 22.1 %collective-permute-start.12 = (f32[448,128]{1,0:T(8,128)S(1)}, f32[448,128]{1,0:T(8,128)S(1)}, u32[]{:S(2)}, u32[]{:S(2)}) collective-permute-start(f32[448,128]{1,0:T(8,128)S(1)} %slice.19), channel_id=1, source_target_pairs={{0,4},{1,5},{2,6},{3,7},{4,0},{5,1},{6,2},{7,3},{8,12},{9,13},{10,... | collective-permute-start | bytes 688136 | tf_op jit(solution)/shard_map/ppermute | solution.py:322
  38.7 4.1 %collective-permute-start.18 = (f32[16,128]{1,0:T(8,128)S(1)}, f32[16,128]{1,0:T(8,128)S(1)}, u32[]{:S(2)}, u32[]{:S(2)}) collective-permute-start(f32[16,128]{1,0:T(8,128)S(1)} %get-tuple-element.25), channel_id=1, source_target_pairs={{0,2},{1,3},{2,0},{3,1},{4,6},{5,7},{6,4},{7,5},{8,10},{9,11},{10,... | collective-permute-start | bytes 24584 | tf_op jit(solution)/shard_map/ppermute | solution.py:315
  40.8 2.5 %collective-permute-start.17 = (f32[16,128]{1,0:T(8,128)S(1)}, f32[16,128]{1,0:T(8,128)S(1)}, u32[]{:S(2)}, u32[]{:S(2)}) collective-permute-start(f32[16,128]{1,0:T(8,128)S(1)} %get-tuple-element.26), channel_id=1, source_target_pairs={{0,1},{1,2},{2,3},{3,0},{4,5},{5,6},{6,7},{7,4},{8,9},{9,10},{10,1... | collective-permute-start | bytes 24584 | tf_op jit(solution)/shard_map/ppermute | solution.py:315
  40.8 2.5 %collective-permute-start.16 = (f32[16,128]{1,0:T(8,128)S(1)}, f32[16,128]{1,0:T(8,128)S(1)}, u32[]{:S(2)}, u32[]{:S(2)}) collective-permute-start(f32[16,128]{1,0:T(8,128)S(1)} %get-tuple-element.27), channel_id=1, source_target_pairs={{0,3},{1,0},{2,1},{3,2},{4,7},{5,4},{6,5},{7,6},{8,11},{9,8},{10,9... | collective-permute-start | bytes 24584 | tf_op jit(solution)/shard_map/ppermute | solution.py:315
  43.3 13.7 %collective-permute-start.19 = (f32[64,128]{1,0:T(8,128)S(1)}, f32[64,128]{1,0:T(8,128)S(1)}, u32[]{:S(2)}, u32[]{:S(2)}) collective-permute-start(f32[64,128]{1,0:T(8,128)S(1)} %pad_maximum_fusion.1.refs_0_), channel_id=1, source_target_pairs={{0,8},{8,0},{16,24},{24,16},{32,40},{40,32},{48,56},{56,48},{64,72... | collective-permute-start | bytes 98312 | tf_op jit(solution)/shard_map/ppermute | solution.py:317
